TPU v7x, 32 devices: a whole 2x2x4 slice. The times are simulated.
32 devices in a mesh: ctx: 4 (over y, core), tp: 8 (over z, x).
Axes of the slice: x: 2, y: 2, z: 4, core: 2. Of those that a mesh axis runs over, the one named last changes fastest.
Arguments:
- queries: bfloat16 [4096, 8192], P(('ctx', 'tp')), may hold values from -16 to 16
- key_tensor: bfloat16 [4096, 1024], P(('ctx', 'tp')), may hold values from -6 to 6
- value_tensor: bfloat16 [4096, 1024], P(('ctx', 'tp')), may hold values from -6 to 6
- output_gradient: bfloat16 [4096, 8192], P(('ctx', 'tp')), may hold values from -6 to 6
- key_blocks: int32 [32, 8], replicated, may hold values from 0 to 31, as said below
- slot_valid: int32 [32, 8], replicated, may hold values from 0 to 1, as said below
Outputs:
- d_q: bfloat16 [4096, 8192], P(('ctx', 'tp'))
- key_gradient: bfloat16 [4096, 1024], P(('ctx', 'tp'))
- value_gradient: bfloat16 [4096, 1024], P(('ctx', 'tp'))
Inputs may be any that keep to these rules, and one draw needn't show every extreme that they name: `key_blocks`: row b names blocks b - 1, b, b + 1 (clamped to the sequence), block 0, then 8 - 4 blocks that differ from one another and from b - 1, b and b + 1. Row 0 is not read. `slot_valid`: the slot of block b itself is 1 in every row; a window slot naming a block below 1 or above 31 is 0, the block 0 slot is 1, and among the random slots a ragged leading part is 1 except where it names block 0.
All inputs are finite; a program needn't handle non-finite values.
Results may differ from a plain program's by a relative error of at most 0.006.
Values may be sent and summed in bfloat16 or wider, within the bound.
A program may use at most 256 MiB of HBM per device.

v0:
```python
import math

import jax
import jax.numpy as jnp
from jax import lax
from jax.sharding import PartitionSpec as P

QUERY_HEADS = 64
KEY_HEADS = 8
HEAD_SIZE = 128
BLOCK_TOKENS = 128
NB = 8
GROUP_SIZE = 8


def passed_along(value, axis, steps):
    count = lax.axis_size(axis)
    pairs = [(source, (source + steps) % count) for source in range(count)]
    return lax.ppermute(value, axis, pairs)


def sparse_turn(packed):
    q_part, o_part, key_part, value_part, live_part = packed
    scaling = 1.0 / math.sqrt(HEAD_SIZE)
    scores = (
        jnp.einsum("pqhgd,pkhd->phgqk", q_part, key_part, preferred_element_type=jnp.float32)
        * scaling
    )
    scores = jnp.where(live_part[:, None, None, None, :], scores, -jnp.inf)
    row_max = jnp.max(scores, axis=-1, keepdims=True)
    raised = jnp.exp(scores - row_max)
    weights = raised / jnp.sum(raised, axis=-1, keepdims=True)
    prob_grad = jnp.einsum(
        "pqhgd,pkhd->phgqk", o_part, value_part, preferred_element_type=jnp.float32
    )
    row_dot = jnp.sum(weights * prob_grad, axis=-1, keepdims=True)
    score_grad = (weights * (prob_grad - row_dot)).astype(jnp.bfloat16)
    rounded_weights = weights.astype(jnp.bfloat16)
    value_grad = jnp.einsum(
        "phgqk,pqhgd->pkhd", rounded_weights, o_part, preferred_element_type=jnp.float32
    )
    key_grad = (
        jnp.einsum("phgqk,pqhgd->pkhd", score_grad, q_part, preferred_element_type=jnp.float32)
        * scaling
    )
    query_grad = (
        jnp.einsum("phgqk,pkhd->pqhgd", score_grad, key_part, preferred_element_type=jnp.float32)
        * scaling
    )
    return (query_grad, key_grad, value_grad)


def stretch_scores(q_rows, o_rows, key_part, value_part):
    scaling = 1.0 / math.sqrt(HEAD_SIZE)
    scores = (
        jnp.einsum("qhgd,khd->hgqk", q_rows, key_part, preferred_element_type=jnp.float32) * scaling
    )
    prob_grad = jnp.einsum("qhgd,khd->hgqk", o_rows, value_part, preferred_element_type=jnp.float32)
    return (scores, prob_grad)


def split_keys(key_span, value_span):
    key_total = key_span.shape[0]
    step_keys = math.gcd(key_total, 2048)
    steps_count = key_total // step_keys
    return (
        key_span.reshape((steps_count, step_keys) + key_span.shape[1:]),
        value_span.reshape((steps_count, step_keys) + value_span.shape[1:]),
    )


def stats_pass(q_rows, o_rows, key_span, value_span):
    key_steps, value_steps = split_keys(key_span, value_span)
    row_shape = (q_rows.shape[1], q_rows.shape[2], q_rows.shape[0])

    def stats_advance(running, packed):
        row_max, row_sum, row_dot = running
        scores, prob_grad = stretch_scores(q_rows, o_rows, packed[0], packed[1])
        new_max = jnp.maximum(row_max, jnp.max(scores, axis=-1))
        factor = jnp.exp(row_max - new_max)
        raised = jnp.exp(scores - new_max[..., None])
        return (
            (
                new_max,
                row_sum * factor + jnp.sum(raised, axis=-1),
                row_dot * factor + jnp.sum(raised * prob_grad, axis=-1),
            ),
            None,
        )

    initial = (
        jnp.full(row_shape, -jnp.inf, jnp.float32),
        jnp.zeros(row_shape, jnp.float32),
        jnp.zeros(row_shape, jnp.float32),
    )
    result, unused = lax.scan(stats_advance, initial, (key_steps, value_steps))
    return result


def grad_pass(q_rows, o_rows, key_span, value_span, row_max, row_sum, row_delta):
    key_steps, value_steps = split_keys(key_span, value_span)
    scaling = 1.0 / math.sqrt(HEAD_SIZE)

    def grad_advance(query_grad, packed):
        key_part, value_part = packed
        scores, prob_grad = stretch_scores(q_rows, o_rows, key_part, value_part)
        weights = jnp.exp(scores - row_max[..., None]) / row_sum[..., None]
        score_grad = (weights * (prob_grad - row_delta[..., None])).astype(jnp.bfloat16)
        rounded_weights = weights.astype(jnp.bfloat16)
        value_grad = jnp.einsum(
            "hgqk,qhgd->khd", rounded_weights, o_rows, preferred_element_type=jnp.float32
        )
        key_grad = (
            jnp.einsum("hgqk,qhgd->khd", score_grad, q_rows, preferred_element_type=jnp.float32)
            * scaling
        )
        query_grad = (
            query_grad
            + jnp.einsum("hgqk,khd->qhgd", score_grad, key_part, preferred_element_type=jnp.float32)
            * scaling
        )
        return (query_grad, (key_grad, value_grad))

    query_grad, grads_steps = lax.scan(
        grad_advance, jnp.zeros(q_rows.shape, jnp.float32), (key_steps, value_steps)
    )
    return (
        query_grad,
        grads_steps[0].reshape(key_span.shape),
        grads_steps[1].reshape(value_span.shape),
    )


def window_terms(terms):
    below = terms[:, :, 0]
    centre = terms[:, :, 1]
    above = terms[:, :, 2]
    blank = jnp.zeros_like(centre)
    from_next = jnp.concatenate([below[:, 1:], blank], axis=1)
    from_prev = jnp.concatenate([blank, above[:, :-1]], axis=1)
    return (centre + from_next + from_prev, above[:, -1], below[:, 0])


def per_device(queries, key_tensor, value_tensor, output_gradient, key_blocks, slot_valid):
    context_length = lax.axis_size("ctx")
    tp_size = lax.axis_size("tp")
    token_count = queries.shape[0]
    local_key_value = KEY_HEADS // context_length
    per_piece = token_count // BLOCK_TOKENS
    length = context_length * tp_size * token_count
    blocks_total = length // BLOCK_TOKENS
    q_heads, o_heads, k_heads, v_heads = (
        lax.all_to_all(
            queries.reshape(token_count, KEY_HEADS, GROUP_SIZE * HEAD_SIZE),
            "ctx",
            split_axis=1,
            concat_axis=0,
            tiled=True,
        ),
        lax.all_to_all(
            output_gradient.reshape(token_count, KEY_HEADS, GROUP_SIZE * HEAD_SIZE),
            "ctx",
            split_axis=1,
            concat_axis=0,
            tiled=True,
        ),
        lax.all_to_all(
            key_tensor.reshape(token_count, KEY_HEADS, HEAD_SIZE),
            "ctx",
            split_axis=1,
            concat_axis=0,
            tiled=True,
        ),
        lax.all_to_all(
            value_tensor.reshape(token_count, KEY_HEADS, HEAD_SIZE),
            "ctx",
            split_axis=1,
            concat_axis=0,
            tiled=True,
        ),
    )
    key_full, value_full = (
        lax.all_gather(
            k_heads.reshape(context_length, token_count, local_key_value, HEAD_SIZE),
            "tp",
            axis=1,
            tiled=True,
        ),
        lax.all_gather(
            v_heads.reshape(context_length, token_count, local_key_value, HEAD_SIZE),
            "tp",
            axis=1,
            tiled=True,
        ),
    )
    key_by_block = key_full.reshape(blocks_total, BLOCK_TOKENS, local_key_value, HEAD_SIZE)
    value_by_block = value_full.reshape(blocks_total, BLOCK_TOKENS, local_key_value, HEAD_SIZE)
    tp_index = lax.axis_index("tp")
    slot_table = lax.dynamic_slice_in_dim(
        key_blocks.reshape(context_length, tp_size * per_piece, NB),
        tp_index * per_piece,
        per_piece,
        1,
    )
    live_table = lax.dynamic_slice_in_dim(
        slot_valid.reshape(context_length, tp_size * per_piece, NB),
        tp_index * per_piece,
        per_piece,
        1,
    )
    block_ids = (jnp.arange(context_length)[:, None] * tp_size + tp_index) * per_piece + jnp.arange(
        per_piece
    )[None, :]
    keep_rows = (block_ids != 0).astype(jnp.bfloat16)
    key_slots = key_by_block[slot_table].reshape(
        context_length, per_piece, NB * BLOCK_TOKENS, local_key_value, HEAD_SIZE
    )
    value_slots = value_by_block[slot_table].reshape(
        context_length, per_piece, NB * BLOCK_TOKENS, local_key_value, HEAD_SIZE
    )
    live_mask = jnp.broadcast_to(
        (live_table > 0)[..., None], (context_length, per_piece, NB, BLOCK_TOKENS)
    ).reshape(context_length, per_piece, NB * BLOCK_TOKENS)
    q_local = q_heads.reshape(
        context_length, per_piece, BLOCK_TOKENS, local_key_value, GROUP_SIZE, HEAD_SIZE
    )
    o_local = (
        o_heads.reshape(
            context_length, per_piece, BLOCK_TOKENS, local_key_value, GROUP_SIZE, HEAD_SIZE
        )
        * keep_rows[:, :, None, None, None, None]
    )
    dq_sparse, dk_slots, dv_slots = lax.map(
        sparse_turn, (q_local, o_local, key_slots, value_slots, live_mask)
    )
    flat_table = slot_table.reshape(context_length * per_piece, NB)
    dk_terms = dk_slots.reshape(
        context_length, per_piece, NB, BLOCK_TOKENS, local_key_value, HEAD_SIZE
    )
    dv_terms = dv_slots.reshape(
        context_length, per_piece, NB, BLOCK_TOKENS, local_key_value, HEAD_SIZE
    )
    far_table = flat_table[:, 3:]
    dk_total = (
        jnp.zeros((blocks_total, BLOCK_TOKENS, local_key_value, HEAD_SIZE), jnp.float32)
        .at[far_table]
        .add(
            dk_terms[:, :, 3:].reshape(
                context_length * per_piece, NB - 3, BLOCK_TOKENS, local_key_value, HEAD_SIZE
            )
        )
        .reshape(length, local_key_value, HEAD_SIZE)
    )
    dv_total = (
        jnp.zeros((blocks_total, BLOCK_TOKENS, local_key_value, HEAD_SIZE), jnp.float32)
        .at[far_table]
        .add(
            dv_terms[:, :, 3:].reshape(
                context_length * per_piece, NB - 3, BLOCK_TOKENS, local_key_value, HEAD_SIZE
            )
        )
        .reshape(length, local_key_value, HEAD_SIZE)
    )
    near_k, upper_k, lower_k = window_terms(dk_terms)
    near_v, upper_v, lower_v = window_terms(dv_terms)
    got_upper_k, got_upper_v = passed_along((upper_k, upper_v), "tp", 1)
    first_dev = tp_index == 0
    got_upper_k = jnp.where(first_dev, jnp.roll(got_upper_k, 1, 0), got_upper_k)
    got_upper_v = jnp.where(first_dev, jnp.roll(got_upper_v, 1, 0), got_upper_v)
    got_lower_k, got_lower_v = passed_along((lower_k, lower_v), "tp", -1)
    last_dev = tp_index == tp_size - 1
    got_lower_k = jnp.where(last_dev, jnp.roll(got_lower_k, -1, 0), got_lower_k)
    got_lower_v = jnp.where(last_dev, jnp.roll(got_lower_v, -1, 0), got_lower_v)
    near_k = near_k.at[:, 0].add(got_upper_k).at[:, -1].add(got_lower_k)
    near_v = near_v.at[:, 0].add(got_upper_v).at[:, -1].add(got_lower_v)
    near_k = near_k.reshape(context_length, token_count, local_key_value, HEAD_SIZE)
    near_v = near_v.reshape(context_length, token_count, local_key_value, HEAD_SIZE)
    q_first = q_heads[:BLOCK_TOKENS].reshape(BLOCK_TOKENS, local_key_value, GROUP_SIZE, HEAD_SIZE)
    o_first = o_heads[:BLOCK_TOKENS].reshape(BLOCK_TOKENS, local_key_value, GROUP_SIZE, HEAD_SIZE)
    key_line = key_full.reshape(length, local_key_value, HEAD_SIZE)
    value_line = value_full.reshape(length, local_key_value, HEAD_SIZE)

    def owner_pass(totals):
        row_max, row_sum, row_dot = stats_pass(q_first, o_first, key_line, value_line)
        dq_whole, dk_whole, dv_whole = grad_pass(
            q_first, o_first, key_line, value_line, row_max, row_sum, row_dot / row_sum
        )
        return (dq_whole, totals[0] + dk_whole, totals[1] + dv_whole)

    def other_pass(totals):
        return (
            jnp.zeros((BLOCK_TOKENS, local_key_value, GROUP_SIZE, HEAD_SIZE), jnp.float32),
            totals[0],
            totals[1],
        )

    dq_first, dk_total, dv_total = lax.cond(
        tp_index == 0, owner_pass, other_pass, (dk_total, dv_total)
    )
    dq_rows = dq_sparse.reshape(
        context_length * token_count, local_key_value, GROUP_SIZE * HEAD_SIZE
    )
    dq_rows = (
        dq_rows.at[:BLOCK_TOKENS]
        .add(dq_first.reshape(BLOCK_TOKENS, local_key_value, GROUP_SIZE * HEAD_SIZE))
        .astype(jnp.bfloat16)
    )
    dk_sum, dv_sum = (
        lax.psum_scatter(
            dk_total.reshape(context_length, tp_size * token_count, local_key_value, HEAD_SIZE),
            "tp",
            scatter_dimension=1,
            tiled=True,
        ),
        lax.psum_scatter(
            dv_total.reshape(context_length, tp_size * token_count, local_key_value, HEAD_SIZE),
            "tp",
            scatter_dimension=1,
            tiled=True,
        ),
    )
    dk_rows = (
        (dk_sum + near_k)
        .reshape(context_length * token_count, local_key_value, HEAD_SIZE)
        .astype(jnp.bfloat16)
    )
    dv_rows = (
        (dv_sum + near_v)
        .reshape(context_length * token_count, local_key_value, HEAD_SIZE)
        .astype(jnp.bfloat16)
    )
    dq_back, key_gradient_back, value_gradient_back = (
        lax.all_to_all(dq_rows, "ctx", split_axis=0, concat_axis=1, tiled=True),
        lax.all_to_all(dk_rows, "ctx", split_axis=0, concat_axis=1, tiled=True),
        lax.all_to_all(dv_rows, "ctx", split_axis=0, concat_axis=1, tiled=True),
    )
    return (
        dq_back.reshape(token_count, QUERY_HEADS * HEAD_SIZE),
        key_gradient_back.reshape(token_count, KEY_HEADS * HEAD_SIZE),
        value_gradient_back.reshape(token_count, KEY_HEADS * HEAD_SIZE),
    )


def solution(mesh):
    in_specs = (
        P(("ctx", "tp"), None),
        P(("ctx", "tp"), None),
        P(("ctx", "tp"), None),
        P(("ctx", "tp"), None),
        P(),
        P(),
    )
    out_specs = (P(("ctx", "tp"), None), P(("ctx", "tp"), None), P(("ctx", "tp"), None))
    return jax.shard_map(
        per_device, mesh=mesh, in_specs=in_specs, out_specs=out_specs, check_vma=False
    )
```

profile of v0, /device:TPU:1, one launch (start us, length us, event | category | flops | bytes accessed | tf_op | source)
XLA Modules:
  0.0 810.7 jit_solution(4834334833025226536)
XLA Ops:
  8.5 9.1 %all_to_all.105 = bf16[128,8,128]{0,2,1:T(8,128)(2,1)S(1)} all-to-all(bf16[128,8,128]{0,2,1:T(8,128)(2,1)S(1)} %bitcast.467), channel_id=1, replica_groups=mesh['ctx'=4,'tp'=8] {'ctx'}, dimensions={1} | all-to-all | bytes 524288 | tf_op jit(solution)/shard_map/all_to_all | solution.py:167
  19.6 8.4 %all_to_all.106 = bf16[128,8,128]{0,2,1:T(8,128)(2,1)S(1)} all-to-all(bf16[128,8,128]{0,2,1:T(8,128)(2,1)S(1)} %bitcast.468), channel_id=1, replica_groups=mesh['ctx'=4,'tp'=8] {'ctx'}, dimensions={1} | all-to-all | bytes 524288 | tf_op jit(solution)/shard_map/all_to_all | solution.py:174
  31.4 4.6 all-to-all-start.1
  36.0 4.1 copy.388
  40.1 20.8 %all-to-all-done.1 = bf16[128,8,1024]{0,2,1:T(8,128)(2,1)S(1)} async-done(((bf16[128,8,1024]{0,2,1:T(8,128)(2,1)}), bf16[128,8,1024]{0,2,1:T(8,128)(2,1)S(1)}, u32[]{:S(2)}, u32[]{:S(2)}) %all-to-all-start.1) | async-done | bytes 2097184 | tf_op jit(solution)/shard_map/all_to_all | solution.py:153
  60.9 5.2 all-to-all-start.3
  72.4 18.7 %all-to-all-done.3 = bf16[128,8,1024]{0,2,1:T(8,128)(2,1)} async-done(((bf16[128,8,1024]{0,2,1:T(8,128)(2,1)}), bf16[128,8,1024]{0,2,1:T(8,128)(2,1)}, u32[]{:S(2)}, u32[]{:S(2)}) %all-to-all-start.3) | async-done | bytes 2097184 | tf_op jit(solution)/shard_map/all_to_all | solution.py:160
  91.1 3.9 copy.389
  106.0 12.0 %all-gather.5.cloned.1.call-done = bf16[4,1024,2,128]{3,1,2,0:T(8,128)(2,1)} async-done(((bf16[4,128,2,128]{3,1,2,0:T(8,128)(2,1)}), bf16[4,1024,2,128]{3,1,2,0:T(8,128)(2,1)}) %all-gather.5.cloned.1.call-update) | async-done | bytes 2097168 | tf_op jit(solution)/shard_map/all_gather | solution.py:189
  122.1 3.2 copy.387
  125.3 115.8 %while.49 = (s32[]{:T(128)}, f32[4,1,128,2,8,128]{2,5,4,3,1,0:T(8,128)}, f32[4,1,1024,2,128]{4,2,3,0,1:T(8,128)}, f32[4,1,1024,2,128]{4,2,3,0,1:T(8,128)}, bf16[...) while((s32[]{:T(128)}, ...), condition=%wide.region_4.5_spmd, body=%wide.region_0.4_spmd.sunk | while | flops 2737301504 | bytes 104432792 | solution.py:233
  131.2 3.7 fusion.126
  134.9 3.1 fusion.127
  142.8 3.5 fusion.129
  146.6 4.7 fusion.130
  160.1 3.7 fusion.126
  163.8 3.1 fusion.127
  171.7 3.5 fusion.129
  175.5 4.7 fusion.130
  189.0 3.7 fusion.126
  192.6 3.1 fusion.127
  200.6 3.5 fusion.129
  204.4 4.7 fusion.130
  217.9 3.7 fusion.126
  221.5 3.1 fusion.127
  229.5 3.5 fusion.129
  233.3 4.7 fusion.130
  245.7 8.4 %scatter_fusion = f32[32,128,2,128]{3,1,2,0:T(8,128)} fusion(f32[32,128,2,128]{3,1,2,0:T(8,128)} %broadcast.235.clone, s32[20]{0:T(128)S(1)} %copy-done.11, f32[20,128,2,128]{3,1,2,0:T(8,128)S(1)} %bitcast.440), kind=kCustom, calls=%fused_computation.2 | custom fusion | flops 655360 | bytes 7864400 | tf_op jit(solution)/shard_map/scatter-add | solution.py:247
  254.0 4.8 copy.399
  261.7 8.0 scatter_fusion.1
  269.7 4.8 copy.402
  274.5 192.8 %conditional.1 = (f32[4096,2,128]{2,1,0:T(2,128)}, f32[4096,2,128]{2,1,0:T(2,128)}, f32[128,2,1024]{2,0,1:T(8,128)}) conditional(s32[]{:T(128)} %convert_element_type.40, (f32[4096,2,128]{2,0,1:T(8,128)}, f32[4096,2,128]{2,0,1:T(8,128)}) %tuple.51, (bf16[4,1024,2,128]{3,1,2,0:T(8,128)(2,1)}, bf16[4,1024,2,128]{3,1,2,0:T(8,128)(2,1)}, ...), branch_computations={%region_7.8_spmd, %region_8.16_spmd} | conditional | flops 7586725888 | bytes 306381536 | solution.py:297
  277.7 3.2 copy.407
  290.5 55.1 %while.47 = (s32[]{:T(128)}, f32[2,8,128]{2,1,0:T(8,128)S(1)}, f32[2,8,128]{2,1,0:T(8,128)S(1)}, f32[2,8,128]{2,1,0:T(8,128)S(1)}, bf16[2,2048,2,128]{3,1,2,0:T(...) while((s32[]{:T(128)}, f32[2,8,128]{2,1,0:T(8,128)S(1)}, ...), condition=%wide.region_13.13_spmd.clone, body=%wide.region_9.12_spmd.clone.sunk | while | flops 2185246720 | bytes 53624956 | solution.py:96
  290.5 9.3 %bitcast_reduce_fusion.5 = (f32[2,8,128]{2,1,0:T(8,128)S(1)}, f32[2,2048,128,8]{2,1,3,0:T(8,128)}) fusion(bf16[128,2,8,128]{3,0,2,1:T(8,128)(2,1)S(1)} %get-tuple-element.855, bf16[2,2048,2,128]{3,1,2,0:T(8,128)(2,1)} %get-tuple-element.854, s32[]{:T(128)S(6)} %copy.517), kind=kOutput, calls=%fused_computation.7.clone.1 | convolution fusion | flops 1082128384 | bytes 18358276 | tf_op jit(solution)/shard_map/cond/branch_1_fun/while/body/eval_jaxpr/qhgd,khd->hgqk/dot_general | solution.py:56
  299.7 9.7 %fusion.134 = f32[2,8,128]{2,1,0:T(8,128)S(1)} fusion(f32[2,2048,128,8]{2,1,3,0:T(8,128)} %get-tuple-element.814, f32[2,8,128]{2,1,0:T(8,128)S(1)} %select_maximum_fusion.2, bf16[128,2,8,128]{3,0,2,1:T(8,128)(2,1)} %get-tuple-element.857, bf16[2,2048,2,128]{3,1,2,0:T(8,128)(2,1)} %get-tuple-element.856, s32[]{:T(128)S(6)} %copy.517), kind=kOutput, calls=%fused_computation.5.clone.1 | convolution fusion | flops 1090516992 | bytes 18366468 | tf_op jit(solution)/shard_map/cond/branch_1_fun/while/body/eval_jaxpr/qhgd,khd->hgqk/dot_general | solution.py:58
  309.4 8.5 %fusion.135 = f32[2,8,128]{2,1,0:T(8,128)S(1)} fusion(f32[2,2048,128,8]{2,1,3,0:T(8,128)} %get-tuple-element.814, f32[2,8,128]{2,1,0:T(8,128)S(1)} %select_maximum_fusion.2), kind=kLoop, calls=%fused_computation.9.clone.1 | loop fusion | flops 12580864 | bytes 16793600 | tf_op jit(solution)/shard_map/cond/branch_1_fun/while/body/eval_jaxpr/reduce_sum | solution.py:85
  318.0 9.3 %bitcast_reduce_fusion.5 = (f32[2,8,128]{2,1,0:T(8,128)S(1)}, f32[2,2048,128,8]{2,1,3,0:T(8,128)}) fusion(bf16[128,2,8,128]{3,0,2,1:T(8,128)(2,1)S(1)} %get-tuple-element.855, bf16[2,2048,2,128]{3,1,2,0:T(8,128)(2,1)} %get-tuple-element.854, s32[]{:T(128)S(6)} %copy.517), kind=kOutput, calls=%fused_computation.7.clone.1 | convolution fusion | flops 1082128384 | bytes 18358276 | tf_op jit(solution)/shard_map/cond/branch_1_fun/while/body/eval_jaxpr/qhgd,khd->hgqk/dot_general | solution.py:56
  327.3 9.7 %fusion.134 = f32[2,8,128]{2,1,0:T(8,128)S(1)} fusion(f32[2,2048,128,8]{2,1,3,0:T(8,128)} %get-tuple-element.814, f32[2,8,128]{2,1,0:T(8,128)S(1)} %select_maximum_fusion.2, bf16[128,2,8,128]{3,0,2,1:T(8,128)(2,1)} %get-tuple-element.857, bf16[2,2048,2,128]{3,1,2,0:T(8,128)(2,1)} %get-tuple-element.856, s32[]{:T(128)S(6)} %copy.517), kind=kOutput, calls=%fused_computation.5.clone.1 | convolution fusion | flops 1090516992 | bytes 18366468 | tf_op jit(solution)/shard_map/cond/branch_1_fun/while/body/eval_jaxpr/qhgd,khd->hgqk/dot_general | solution.py:58
  337.0 8.5 %fusion.135 = f32[2,8,128]{2,1,0:T(8,128)S(1)} fusion(f32[2,2048,128,8]{2,1,3,0:T(8,128)} %get-tuple-element.814, f32[2,8,128]{2,1,0:T(8,128)S(1)} %select_maximum_fusion.2), kind=kLoop, calls=%fused_computation.9.clone.1 | loop fusion | flops 12580864 | bytes 16793600 | tf_op jit(solution)/shard_map/cond/branch_1_fun/while/body/eval_jaxpr/reduce_sum | solution.py:85
  345.6 102.4 %while.48 = (s32[]{:T(128)}, f32[128,2,8,128]{0,3,2,1:T(8,128)}, f32[2,2048,2,128]{3,2,1,0:T(2,128)}, f32[2,2048,2,128]{3,2,1,0:T(2,128)}, bf16[2,2048,2,128]{3,...) while((s32[]{:T(128)}, f32[128,2,8,128]{0,3,2,1:T(8,128)}, ...), condition=%wide.region_15.15_spmd.clone, body=%wide.region_14.14_spmd.clone.sunk | while | flops 5399379968 | bytes 187720016 | solution.py:124
  345.8 8.6 %fusion.147 = f32[2,8,128,2048]{2,3,1,0:T(8,128)} fusion(f32[2,8,128]{2,1,0:T(8,128)S(1)} %get-tuple-element.893, f32[2,8,128]{2,1,0:T(8,128)S(1)} %get-tuple-element.892, bf16[128,2,8,128]{3,0,2,1:T(8,128)(2,1)S(1)} %get-tuple-element.891, bf16[2,2048,2,128]{3,1,2,0:T(8,128)(2,1)} %get-tuple-element.890, s32[]{:T(128)S(6)} %copy.529), kind=kOutput, calls=%fused_computation.28.clone.1 | convolution fusion | flops 1086324736 | bytes 18366468 | tf_op jit(solution)/shard_map/cond/branch_1_fun/while/body/eval_jaxpr/qhgd,khd->hgqk/dot_general | solution.py:56
  354.4 11.9 %fusion.148 = bf16[2,8,128,2048]{2,3,1,0:T(8,128)(2,1)} fusion(f32[2,8,128,2048]{2,3,1,0:T(8,128)} %fusion.147, f32[2,8,128]{2,1,0:T(8,128)S(1)} %get-tuple-element.896, bf16[128,2,8,128]{3,0,2,1:T(8,128)(2,1)} %get-tuple-element.895, bf16[2,2048,2,128]{3,1,2,0:T(8,128)(2,1)} %get-tuple-element.894, s32[]{:T(128)S(6)} %copy.529), kind=kOutput, calls=%fused_computation.25.clone.1 | convolution fusion | flops 1086324736 | bytes 26746884 | tf_op jit(solution)/shard_map/cond/branch_1_fun/while/body/eval_jaxpr/qhgd,khd->hgqk/dot_general | solution.py:58
  366.3 6.2 fusion.149
  372.5 8.4 %fusion.150 = f32[1,2048,2,128]{3,1,2,0:T(8,128)S(1)} fusion(bf16[128,2,8,128]{3,0,2,1:T(8,128)(2,1)} %get-tuple-element.895, f32[2,8,128,2048]{2,3,1,0:T(8,128)} %fusion.147), kind=kOutput, calls=%fused_computation.31.clone.1 | convolution fusion | flops 1077936128 | bytes 19398656 | tf_op jit(solution)/shard_map/cond/branch_1_fun/while/body/eval_jaxpr/hgqk,qhgd->khd/dot_general | solution.py:110
  384.4 9.1 %copy_dynamic-update-slice_fusion.3 = (f32[2,2048,2,128]{3,2,1,0:T(2,128)S(1)}, f32[2,2048,2,128]{3,2,1,0:T(2,128)S(1)}) fusion(f32[2,2048,2,128]{3,2,1,0:T(2,128)S(1)} %copy-done.8, s32[]{:T(128)S(6)} %copy.529, f32[1,2048,2,128]{3,1,2,0:T(8,128)S(1)} %fusion.150, f32[2,2048,2,128]{3,2,1,0:T(2,128)S(1)} %copy-done.6, f32[1,2048,2,128]{3,1,2,0:T(8,128)S(1)} %fusion.151), kind=kLoop, calls=%fused_computation.35.clone.1 | loop fusion | bytes 8388612 | tf_op jit(solution)/shard_map/cond/branch_1_fun/while/body/jit(dynamic_update_index_in_dim)/dynamic_update_slice | solution.py:124
  396.8 8.6 %fusion.147 = f32[2,8,128,2048]{2,3,1,0:T(8,128)} fusion(f32[2,8,128]{2,1,0:T(8,128)S(1)} %get-tuple-element.893, f32[2,8,128]{2,1,0:T(8,128)S(1)} %get-tuple-element.892, bf16[128,2,8,128]{3,0,2,1:T(8,128)(2,1)S(1)} %get-tuple-element.891, bf16[2,2048,2,128]{3,1,2,0:T(8,128)(2,1)} %get-tuple-element.890, s32[]{:T(128)S(6)} %copy.529), kind=kOutput, calls=%fused_computation.28.clone.1 | convolution fusion | flops 1086324736 | bytes 18366468 | tf_op jit(solution)/shard_map/cond/branch_1_fun/while/body/eval_jaxpr/qhgd,khd->hgqk/dot_general | solution.py:56
  405.4 11.9 %fusion.148 = bf16[2,8,128,2048]{2,3,1,0:T(8,128)(2,1)} fusion(f32[2,8,128,2048]{2,3,1,0:T(8,128)} %fusion.147, f32[2,8,128]{2,1,0:T(8,128)S(1)} %get-tuple-element.896, bf16[128,2,8,128]{3,0,2,1:T(8,128)(2,1)} %get-tuple-element.895, bf16[2,2048,2,128]{3,1,2,0:T(8,128)(2,1)} %get-tuple-element.894, s32[]{:T(128)S(6)} %copy.529), kind=kOutput, calls=%fused_computation.25.clone.1 | convolution fusion | flops 1086324736 | bytes 26746884 | tf_op jit(solution)/shard_map/cond/branch_1_fun/while/body/eval_jaxpr/qhgd,khd->hgqk/dot_general | solution.py:58
  417.3 6.4 fusion.149
  423.7 8.4 %fusion.150 = f32[1,2048,2,128]{3,1,2,0:T(8,128)S(1)} fusion(bf16[128,2,8,128]{3,0,2,1:T(8,128)(2,1)} %get-tuple-element.895, f32[2,8,128,2048]{2,3,1,0:T(8,128)} %fusion.147), kind=kOutput, calls=%fused_computation.31.clone.1 | convolution fusion | flops 1077936128 | bytes 19398656 | tf_op jit(solution)/shard_map/cond/branch_1_fun/while/body/eval_jaxpr/hgqk,qhgd->khd/dot_general | solution.py:110
  435.6 9.1 %copy_dynamic-update-slice_fusion.3 = (f32[2,2048,2,128]{3,2,1,0:T(2,128)S(1)}, f32[2,2048,2,128]{3,2,1,0:T(2,128)S(1)}) fusion(f32[2,2048,2,128]{3,2,1,0:T(2,128)S(1)} %copy-done.8, s32[]{:T(128)S(6)} %copy.529, f32[1,2048,2,128]{3,1,2,0:T(8,128)S(1)} %fusion.150, f32[2,2048,2,128]{3,2,1,0:T(2,128)S(1)} %copy-done.6, f32[1,2048,2,128]{3,1,2,0:T(8,128)S(1)} %fusion.151), kind=kLoop, calls=%fused_computation.35.clone.1 | loop fusion | bytes 8388612 | tf_op jit(solution)/shard_map/cond/branch_1_fun/while/body/jit(dynamic_update_index_in_dim)/dynamic_update_slice | solution.py:124
  448.0 16.5 %bitcast_add_fusion = (f32[4096,2,128]{2,1,0:T(2,128)}, f32[4096,2,128]{2,1,0:T(2,128)}) fusion(f32[2,2048,2,128]{3,2,1,0:T(2,128)} %get-tuple-element.236, f32[4096,2,128]{2,0,1:T(8,128)} %get-tuple-element.552, f32[2,2048,2,128]{3,2,1,0:T(2,128)} %get-tuple-element.234, f32[4096,2,128]{2,0,1:T(8,128)} %get-tuple-element.551), kind=kLoop, calls=%fused_computation.49 | loop fusion | flops 2097152 | bytes 25165824 | tf_op jit(solution)/shard_map/cond/branch_1_fun/add | solution.py:288
  467.3 6.9 copy.416
  474.2 6.9 copy.425
  481.1 3.8 copy.395
  491.3 5.1 copy.412
  496.4 5.5 all-to-all-start.4
  504.2 4.2 collective-permute-start.1
  510.7 4.2 collective-permute-start.3
  516.1 16.4 %collective-permute-done = f32[4,128,2,128]{3,1,2,0:T(8,128)} collective-permute-done((f32[4,128,2,128]{3,1,2,0:T(8,128)}, f32[4,128,2,128]{3,1,2,0:T(8,128)}, u32[]{:S(2)}, u32[]{:S(2)}) %collective-permute-start) | collective-permute-done | bytes 524320 | tf_op jit(solution)/shard_map/ppermute | solution.py:19
  539.2 15.7 %collective-permute-done.2 = f32[4,128,2,128]{3,1,2,0:T(8,128)S(1)} collective-permute-done((f32[4,128,2,128]{3,1,2,0:T(8,128)}, f32[4,128,2,128]{3,1,2,0:T(8,128)S(1)}, u32[]{:S(2)}, u32[]{:S(2)}) %collective-permute-start.2) | collective-permute-done | bytes 524320 | tf_op jit(solution)/shard_map/ppermute | solution.py:19
  557.6 215.2 %all-reduce.5.cloned.1.call-done = (f32[4,1024,2,128]{3,0,2,1:T(4,128)}, f32[4,1024,2,128]{3,0,2,1:T(4,128)}) async-done(((f32[4,1024,2,128]{3,0,2,1:T(4,128)}, f32[4,1024,2,128]{3,0,2,1:T(4,128)}), (f32[4,1024,2,128]{3,0,2,1:T(4,128)}, f32[4,1024,2,128]{3,0,2,1:T(4,128)})) %all-reduce.5.cloned.1.call-update) | async-done | bytes 8388624
  778.6 4.7 all-to-all-start.5
  788.6 4.2 all-to-all-start.6
  (196 shorter events, 162.3 us)
Async XLA Ops:
  7.2 21.8 %copy-start.10 = (bf16[128,8192]{1,0:T(8,128)(2,1)S(1)}, bf16[128,8192]{1,0:T(8,128)(2,1)}, u32[]{:S(2)}) copy-start(bf16[128,8192]{1,0:T(8,128)(2,1)} %param.24) | copy-start | bytes 6291460
  7.2 91.7 %all-gather.3.cloned.1.call-start = ((), (), s32[]{:S(2)}) async-start(), calls=%async_computation.7 | async-start | bytes 2359296 | tf_op jit(solution)/shard_map/all_gather | solution.py:183
  18.4 99.6 %all-gather.5.cloned.1.call-start = ((), (), s32[]{:S(2)}) async-start(), calls=%async_computation.8 | async-start | bytes 2359296 | tf_op jit(solution)/shard_map/all_gather | solution.py:189
  31.4 29.6 %all-to-all-start.1 = ((bf16[128,8,1024]{0,2,1:T(8,128)(2,1)}), bf16[128,8,1024]{0,2,1:T(8,128)(2,1)S(1)}, u32[]{:S(2)}, u32[]{:S(2)}) async-start(bf16[128,8,1024]{0,2,1:T(8,128)(2,1)} %bitcast.442), calls=%async_computation.1 | async-start | bytes 4194304 | tf_op jit(solution)/shard_map/all_to_all | solution.py:153
  36.0 30.1 %copy-start.12 = (s32[32,8]{0,1:T(8,128)S(1)}, s32[32,8]{0,1:T(8,128)}, u32[]{:S(2)}) copy-start(s32[32,8]{0,1:T(8,128)} %param.29) | copy-start | bytes 3076
  36.0 30.2 %copy-start.13 = (s32[32,8]{0,1:T(8,128)S(1)}, s32[32,8]{0,1:T(8,128)}, u32[]{:S(2)}) copy-start(s32[32,8]{0,1:T(8,128)} %param.28) | copy-start | bytes 3076
  60.9 6.6 copy-start.4
  60.9 30.1 %all-to-all-start.3 = ((bf16[128,8,1024]{0,2,1:T(8,128)(2,1)}), bf16[128,8,1024]{0,2,1:T(8,128)(2,1)}, u32[]{:S(2)}, u32[]{:S(2)}) async-start(bf16[128,8,1024]{0,2,1:T(8,128)(2,1)} %bitcast.441), calls=%async_computation.3 | async-start | bytes 4194304 | tf_op jit(solution)/shard_map/all_to_all | solution.py:160
  66.1 706.8 %all-reduce.5.cloned.1.call-start = ((), (), s32[]{:S(2)}) async-start(), calls=%async_computation.9 | async-start | bytes 16777216
  70.4 24.6 %copy-start.1 = (bf16[128,8,1024]{2,0,1:T(8,128)(2,1)}, bf16[128,8,1024]{2,0,1:T(8,128)(2,1)S(1)}, u32[]{:S(2)}) copy-start(bf16[128,8,1024]{2,0,1:T(8,128)(2,1)S(1)} %copy.382) | copy-start | bytes 6291460
  138.0 2.0 copy-start
  166.9 2.0 copy-start
  195.8 2.0 copy-start
  224.7 2.0 copy-start
  243.0 2.7 copy-start.11
  254.0 4.8 copy-start.5
  269.7 4.8 copy-start.2
  282.3 3.4 copy-start.3
  366.3 14.6 %slice-start = ((s8[8388608]{0:T(1024)(128)(4,1)}), s8[4194304]{0:T(1024)(128)(4,1)S(1)}, s32[]{:S(2)}) async-start(s8[8388608]{0:T(1024)(128)(4,1)} %bitcast.433), calls=%async_computation.10 | async-start | bytes 8388608 | tf_op jit(solution)/shard_map/cond/branch_1_fun/while
  372.5 8.4 %slice-start.1 = ((s8[8388608]{0:T(1024)(128)(4,1)}), s8[4194304]{0:T(1024)(128)(4,1)S(1)}, s32[]{:S(2)}) async-start(s8[8388608]{0:T(1024)(128)(4,1)} %bitcast.433), calls=%async_computation.11 | async-start | bytes 8388608 | tf_op jit(solution)/shard_map/cond/branch_1_fun/while
  380.9 2.4 copy-start.6
  380.9 3.5 copy-start.8
  393.5 1.9 copy-start.7
  393.5 3.3 copy-start.9
  417.3 14.8 %slice-start = ((s8[8388608]{0:T(1024)(128)(4,1)}), s8[4194304]{0:T(1024)(128)(4,1)S(1)}, s32[]{:S(2)}) async-start(s8[8388608]{0:T(1024)(128)(4,1)} %bitcast.433), calls=%async_computation.10 | async-start | bytes 8388608 | tf_op jit(solution)/shard_map/cond/branch_1_fun/while
  423.7 8.4 %slice-start.1 = ((s8[8388608]{0:T(1024)(128)(4,1)}), s8[4194304]{0:T(1024)(128)(4,1)S(1)}, s32[]{:S(2)}) async-start(s8[8388608]{0:T(1024)(128)(4,1)} %bitcast.433), calls=%async_computation.11 | async-start | bytes 8388608 | tf_op jit(solution)/shard_map/cond/branch_1_fun/while
  432.1 2.4 copy-start.6
  432.1 3.5 copy-start.8
  444.7 1.9 copy-start.7
  444.8 3.3 copy-start.9
  496.4 18.5 %copy-start.14 = (u32[32]{0:T(128)S(1)}, u32[32]{0:T(128)}, u32[]{:S(2)}) copy-start(u32[32]{0:T(128)} %constant.190) | copy-start | bytes 388
  496.4 282.2 %all-to-all-start.4 = ((bf16[512,2,1024]{2,1,0:T(2,128)(2,1)}), bf16[512,2,1024]{2,1,0:T(2,128)(2,1)S(1)}, u32[]{:S(2)}, u32[]{:S(2)}) async-start(bf16[512,2,1024]{2,1,0:T(2,128)(2,1)} %copy.412), calls=%async_computation.4 | async-start | bytes 4194304 | tf_op jit(solution)/shard_map/all_to_all | solution.py:333
  504.2 28.3 %collective-permute-start = (f32[4,128,2,128]{3,1,2,0:T(8,128)}, f32[4,128,2,128]{3,1,2,0:T(8,128)}, u32[]{:S(2)}, u32[]{:S(2)}) collective-permute-start(f32[4,128,2,128]{3,1,2,0:T(8,128)} %get-tuple-element.632), channel_id=1, source_target_pairs={{0,1},{1,2},{2,3},{3,4},{4,5},{5,6},{6,7},{7,0},{8,9},{9,10},{10,1... | collective-permute-start | bytes 1572872 | tf_op jit(solution)/shard_map/ppermute | solution.py:19
  504.2 31.6 %collective-permute-start.1 = (f32[4,128,2,128]{3,1,2,0:T(8,128)}, f32[4,128,2,128]{3,1,2,0:T(8,128)}, u32[]{:S(2)}, u32[]{:S(2)}) collective-permute-start(f32[4,128,2,128]{3,1,2,0:T(8,128)} %get-tuple-element.631), channel_id=1, source_target_pairs={{0,7},{1,0},{2,1},{3,2},{4,3},{5,4},{6,5},{7,6},{8,15},{9,8},{10,9... | collective-permute-start | bytes 1572872 | tf_op jit(solution)/shard_map/ppermute | solution.py:19
  510.7 44.2 %collective-permute-start.2 = (f32[4,128,2,128]{3,1,2,0:T(8,128)}, f32[4,128,2,128]{3,1,2,0:T(8,128)S(1)}, u32[]{:S(2)}, u32[]{:S(2)}) collective-permute-start(f32[4,128,2,128]{3,1,2,0:T(8,128)} %get-tuple-element.630), channel_id=1, source_target_pairs={{0,1},{1,2},{2,3},{3,4},{4,5},{5,6},{6,7},{7,0},{8,9},{9,10},{10,1... | collective-permute-start | bytes 1572872 | tf_op jit(solution)/shard_map/ppermute | solution.py:19
  510.7 45.5 %collective-permute-start.3 = (f32[4,128,2,128]{3,1,2,0:T(8,128)}, f32[4,128,2,128]{3,1,2,0:T(8,128)S(1)}, u32[]{:S(2)}, u32[]{:S(2)}) collective-permute-start(f32[4,128,2,128]{3,1,2,0:T(8,128)} %get-tuple-element.629), channel_id=1, source_target_pairs={{0,7},{1,0},{2,1},{3,2},{4,3},{5,4},{6,5},{7,6},{8,15},{9,8},{10,9... | collective-permute-start | bytes 1572872 | tf_op jit(solution)/shard_map/ppermute | solution.py:19
  778.6 10.0 %all-to-all-start.5 = ((bf16[512,2,128]{2,1,0:T(2,128)(2,1)}), bf16[512,2,128]{2,1,0:T(2,128)(2,1)}, u32[]{:S(2)}, u32[]{:S(2)}) async-start(bf16[512,2,128]{2,1,0:T(2,128)(2,1)} %copy.421), calls=%async_computation.5 | async-start | bytes 524288 | tf_op jit(solution)/shard_map/all_to_all | solution.py:334
  788.6 14.1 %all-to-all-start.6 = ((bf16[512,2,128]{2,1,0:T(2,128)(2,1)}), bf16[512,2,128]{2,1,0:T(2,128)(2,1)S(1)}, u32[]{:S(2)}, u32[]{:S(2)}) async-start(bf16[512,2,128]{2,1,0:T(2,128)(2,1)} %copy.431), calls=%async_computation.6 | async-start | bytes 524288 | tf_op jit(solution)/shard_map/all_to_all | solution.py:335
Sparse Core Ops, SparseCore 0:
  18.6 48.8 all-gather.2
  70.2 47.7 all-gather.4
  481.2 291.5 all-reduce.4
where the time goes:
time: 819 us; the launch traced here: 811 us
  waiting for transfers between devices  302 us (37%)
  local copies, waits for them, and re-layouts  182 us (22%)
  matrix products  181 us (22%)
  other arithmetic  79 us (10%)
  starting transfers between devices  32.7 us (4%)
  blocking collectives  17.5 us (2%)
  between operations  15 us (2%)
    unnamed x4, waiting for transfers between devices  215 us
    dot_general x4, matrix products, stretch_scores(): jnp.einsum('qhgd,khd->hgqk', o_rows, value_part, preferred_element_type=j...  43.2 us
    dot_general x4, matrix products, stretch_scores(): jnp.einsum('qhgd,khd->hgqk', q_rows, key_part, preferred_element_type=jnp...  35.8 us
    ppermute x4, waiting for transfers between devices, passed_along(): return lax.ppermute(value, axis, pairs)  32.7 us
    unnamed x32, local copies, waits for them, and re-layouts  21.4 us
    all_to_all x1, waiting for transfers between devices, per_device(): lax.all_to_all(queries.reshape(token_count, KEY_HEADS, GROUP_SIZE * HEAD_...  20.8 us
    dot_general x4, matrix products, sparse_turn(): jnp.einsum('phgqk,pqhgd->pkhd', score_grad, q_part, preferred_element_typ...  18.7 us
    all_to_all x1, waiting for transfers between devices, per_device(): lax.all_to_all(output_gradient.reshape(token_count, KEY_HEADS, GROUP_SIZE...  18.7 us
  transfers between devices with their start and end apart: 12, of which 8 were waited for; matrix products, arithmetic and copies ran while one was open for 10% of the time, Pallas kernels for 0%

commit v1 on v0

v1 whole, which is shorter than its diff:
```python
import functools
import math

import jax
import jax.numpy as jnp
from jax import lax
from jax.experimental import pallas as pl
from jax.experimental.pallas import tpu as pltpu
from jax.sharding import PartitionSpec as P

KEY_HEADS = 8
HEAD_SIZE = 128
BLOCK_TOKENS = 128
NB = 8
GROUP_SIZE = 8

SCALE = 1.0 / math.sqrt(HEAD_SIZE)
LOG_SCALE = SCALE * math.log2(math.e)
T = BLOCK_TOKENS
D = HEAD_SIZE
F32 = jnp.float32
BF16 = jnp.bfloat16


def dot_nt(a, b):
    return lax.dot_general(a, b, (((1,), (1,)), ((), ())), preferred_element_type=F32)


def dot_nn(a, b):
    return jnp.dot(a, b, preferred_element_type=F32)


def grad_kernel(
    table, live, keep,
    q_ref, o_ref, k_ref, v_ref, qd_ref, od_ref,
    dq_ref, dk_ref, dv_ref, dqd_ref,
    kt, acc_k, acc_v, qs, os_, kg, vg, ktg, s_buf, g_buf, pb, ds,
):
    j = pl.program_id(1)
    length = k_ref.shape[0]
    chunk = math.gcd(length, 512)

    @pl.when(j == 0)
    def dense():
        qd = qd_ref[...]
        od = od_ref[...]
        rows = qd.shape[0]

        def stats(i, carry):
            m, l, dl = carry
            at = pl.multiple_of(i * chunk, chunk)
            k = k_ref[pl.ds(at, chunk), :]
            s = dot_nt(k, qd) * LOG_SCALE
            g = dot_nt(v_ref[pl.ds(at, chunk), :], od)
            kt[:, pl.ds(at, chunk)] = k.T
            m_new = jnp.maximum(m, jnp.max(s, axis=0, keepdims=True))
            f = jnp.exp2(m - m_new)
            p = jnp.exp2(s - m_new)
            l = l * f + jnp.sum(p, axis=0, keepdims=True)
            dl = dl * f + jnp.sum(p * g, axis=0, keepdims=True)
            return m_new, l, dl

        m, l, dl = lax.fori_loop(
            0, length // chunk, stats,
            (jnp.full((1, rows), -1e30, F32), jnp.zeros((1, rows), F32), jnp.zeros((1, rows), F32)),
        )
        rl = 1.0 / l
        delta = dl * rl

        def grads(i, dqt):
            at = pl.multiple_of(i * chunk, chunk)
            s = dot_nt(k_ref[pl.ds(at, chunk), :], qd) * LOG_SCALE
            g = dot_nt(v_ref[pl.ds(at, chunk), :], od)
            p = jnp.exp2(s - m) * rl
            d = (p * (g - delta)).astype(BF16)
            acc_v[pl.ds(at, chunk), :] = dot_nn(p.astype(BF16), od)
            acc_k[pl.ds(at, chunk), :] = dot_nn(d, qd)
            return dqt + dot_nn(kt[:, pl.ds(at, chunk)], d)

        dqt = lax.fori_loop(0, length // chunk, grads, jnp.zeros((D, rows), F32))
        dqd_ref[...] = (dqt * SCALE).T.astype(BF16)

    @pl.when(keep[j] == 0)
    def blank():
        dq_ref[...] = jnp.zeros_like(dq_ref)

    @pl.when(keep[j] != 0)
    def sparse():
        for g in range(GROUP_SIZE):
            qs[g * T:(g + 1) * T, :] = q_ref[:, g * D:(g + 1) * D]
            os_[g * T:(g + 1) * T, :] = o_ref[:, g * D:(g + 1) * D]
        bias = []
        for s in range(NB):
            at = pl.multiple_of(table[j * NB + s] * T, T)
            kg[s * T:(s + 1) * T, :] = k_ref[pl.ds(at, T), :]
            vg[s * T:(s + 1) * T, :] = v_ref[pl.ds(at, T), :]
            ktg[:, s * T:(s + 1) * T] = kt[:, pl.ds(at, T)]
            bias.append(jnp.where(live[j * NB + s] > 0, 0.0, -1e30).astype(F32))
        R = 2 * T
        for pair in range(GROUP_SIZE // 2):
            q2 = qs[pair * R:(pair + 1) * R, :]
            o2 = os_[pair * R:(pair + 1) * R, :]
            m = None
            for s in range(NB):
                sc = dot_nt(kg[s * T:(s + 1) * T, :], q2)
                s_buf[s * T:(s + 1) * T, :] = sc
                top = jnp.max(sc, axis=0, keepdims=True) * LOG_SCALE + bias[s]
                m = top if m is None else jnp.maximum(m, top)
            l = jnp.zeros((1, R), F32)
            dl = jnp.zeros((1, R), F32)
            for s in range(NB):
                rows = slice(s * T, (s + 1) * T)
                p = jnp.exp2(s_buf[rows, :] * LOG_SCALE - (m - bias[s]))
                g = dot_nt(vg[rows, :], o2)
                l = l + jnp.sum(p, axis=0, keepdims=True)
                dl = dl + jnp.sum(p * g, axis=0, keepdims=True)
                s_buf[rows, :] = p
                g_buf[rows, :] = g
            rl = 1.0 / l
            delta = dl * rl
            cols = slice(pair * R, (pair + 1) * R)
            for s in range(NB):
                rows = slice(s * T, (s + 1) * T)
                p = s_buf[rows, :] * rl
                pb[rows, cols] = p.astype(BF16)
                ds[rows, cols] = (p * (g_buf[rows, :] - delta)).astype(BF16)
            dqt = dot_nn(ktg[...], ds[:, cols]) * SCALE
            dq_ref[:, 2 * pair * D:(2 * pair + 1) * D] = dqt[:, :T].T.astype(BF16)
            dq_ref[:, (2 * pair + 1) * D:(2 * pair + 2) * D] = dqt[:, T:].T.astype(BF16)
        for s in range(NB):
            rows = slice(s * T, (s + 1) * T)
            at = pl.multiple_of(table[j * NB + s] * T, T)
            acc_v[pl.ds(at, T), :] += dot_nn(pb[rows, :], os_[...])
            acc_k[pl.ds(at, T), :] += dot_nn(ds[rows, :], qs[...])

    @pl.when(j == pl.num_programs(1) - 1)
    def finish():
        dk_ref[...] = (acc_k[...] * SCALE).astype(BF16)
        dv_ref[...] = acc_v[...].astype(BF16)


def gradients(table, live, keep, q, o, kv, qd, od):
    blocks = table.shape[0]
    length = kv.shape[0]
    heads = kv.shape[1] // (2 * D)
    rows = qd.shape[0]
    wide = GROUP_SIZE * D
    spec = lambda shape, index: pl.BlockSpec(shape, index)
    row_block = spec((T, wide), lambda h, j, *_: (j, h))
    once = pl.Buffered(1) if heads == 1 else None
    fixed = lambda index: pl.BlockSpec((length, D), index, pipeline_mode=once)
    dense = spec((rows, D), lambda h, j, *_: (0, h))
    return pl.pallas_call(
        grad_kernel,
        grid_spec=pltpu.PrefetchScalarGridSpec(
            num_scalar_prefetch=3,
            grid=(heads, blocks),
            in_specs=[
                row_block, row_block,
                fixed(lambda h, j, *_: (0, h)),
                fixed(lambda h, j, *_: (0, heads + h)),
                dense, dense,
            ],
            out_specs=[
                row_block,
                spec((length, D), lambda h, j, *_: (0, h)),
                spec((length, D), lambda h, j, *_: (0, h)),
                dense,
            ],
            scratch_shapes=[
                pltpu.VMEM((D, length), BF16),
                pltpu.VMEM((length, D), F32),
                pltpu.VMEM((length, D), F32),
                pltpu.VMEM((wide, D), BF16),
                pltpu.VMEM((wide, D), BF16),
                pltpu.VMEM((NB * T, D), BF16),
                pltpu.VMEM((NB * T, D), BF16),
                pltpu.VMEM((D, NB * T), BF16),
                pltpu.VMEM((NB * T, 2 * T), F32),
                pltpu.VMEM((NB * T, 2 * T), F32),
                pltpu.VMEM((NB * T, wide), BF16),
                pltpu.VMEM((NB * T, wide), BF16),
            ],
        ),
        out_shape=[
            jax.ShapeDtypeStruct(q.shape, BF16),
            jax.ShapeDtypeStruct((length, heads * D), BF16),
            jax.ShapeDtypeStruct((length, heads * D), BF16),
            jax.ShapeDtypeStruct(qd.shape, BF16),
        ],
        compiler_params=pltpu.CompilerParams(
            dimension_semantics=("arbitrary", "arbitrary"),
            vmem_limit_bytes=60 * 1024 * 1024,
        ),
        cost_estimate=pl.CostEstimate(
            flops=10 * heads * (blocks + 1) * (wide * NB * T * D),
            bytes_accessed=4 * q.size * 2 + 4 * kv.size * 2,
            transcendentals=heads * (blocks + 1) * wide * NB * T,
        ),
    )(table.reshape(-1), live.reshape(-1), keep, q, o, kv, kv, qd, od)


def tables(key_blocks, slot_valid, ctx, tp, pieces):
    t = lax.axis_index("tp")
    pick = lambda a: lax.dynamic_slice_in_dim(
        a.reshape(ctx, tp * pieces, NB), t * pieces, pieces, 1
    ).reshape(ctx * pieces, NB)
    blocks = pick(key_blocks)
    owner = blocks // pieces
    place = ((owner % tp) * ctx + owner // tp) * pieces + blocks % pieces
    number = jnp.arange(ctx * pieces)
    own = ((number // pieces) * tp + t) * pieces + number % pieces
    return place.astype(jnp.int32), pick(slot_valid), (own != 0).astype(jnp.int32)


def per_device(queries, key_tensor, value_tensor, output_gradient, key_blocks, slot_valid):
    ctx = lax.axis_size("ctx")
    tp = lax.axis_size("tp")
    tokens = queries.shape[0]
    pieces = tokens // T
    heads = KEY_HEADS // ctx
    rows = GROUP_SIZE * T // tp
    wide = GROUP_SIZE * D
    tp_index = lax.axis_index("tp")
    swap = functools.partial(lax.all_to_all, axis_name="ctx", tiled=True)
    kv = jnp.concatenate(
        [key_tensor.reshape(tokens, ctx, heads * D), value_tensor.reshape(tokens, ctx, heads * D)], axis=2
    ).reshape(tokens, ctx * 2 * heads * D)
    kv = swap(kv, split_axis=1, concat_axis=0)
    kv = lax.all_gather(kv, "tp", axis=0, tiled=True)
    q = swap(queries, split_axis=1, concat_axis=0)
    o = swap(output_gradient, split_axis=1, concat_axis=0)

    def spread(a):
        a = a[:T].reshape(T, heads, GROUP_SIZE, D).transpose(2, 0, 1, 3).reshape(GROUP_SIZE * T, heads * D)
        return lax.all_to_all(a, "tp", split_axis=0, concat_axis=0, tiled=True)[:rows]

    table, live, keep = tables(key_blocks, slot_valid, ctx, tp, pieces)
    dq, dk, dv, dqd = gradients(table, live, keep, q, o, kv, spread(q), spread(o))
    first = lax.all_gather(dqd, "tp", axis=0, tiled=True)
    first = first.reshape(GROUP_SIZE, T, heads, D).transpose(1, 2, 0, 3).reshape(T, heads * wide)
    dq = lax.dynamic_update_slice(dq, jnp.where(tp_index == 0, first, dq[:T]), (0, 0))
    back = lambda a: swap(a, split_axis=0, concat_axis=1)

    def collect(a):
        a = lax.all_to_all(a, "tp", split_axis=0, concat_axis=0, tiled=True)
        return jnp.sum(a.reshape(tp, ctx * tokens, heads * D).astype(F32), axis=0).astype(BF16)

    return back(dq), back(collect(dk)), back(collect(dv))


def solution(mesh):
    rows = P(("ctx", "tp"), None)
    return jax.shard_map(
        per_device,
        mesh=mesh,
        in_specs=(rows, rows, rows, rows, P(), P()),
        out_specs=(rows, rows, rows),
        check_vma=False,
    )
```

time: 819 us -> 371 us (0.45)
  waiting for transfers between devices: 302 us -> 111 us
  matrix products: 181 us -> 0 us
  local copies, waits for them, and re-layouts: 182 us -> 27.8 us
  blocking collectives: 17.5 us -> 133 us
  other arithmetic: 79 us -> 5.04 us
  Pallas kernels: 0 us -> 44 us
    unnamed x4 -> x1, waiting for transfers between devices: 215 us -> 0.02 us
    dot_general x34 -> x0, matrix products: 181 us -> none  [the longest x4 43.2 us: stretch_scores(): jnp.einsum('qhgd,khd->hgqk', o_rows, value_part, preferred_element_type=j...]
    all_to_all x2 -> x3, blocking collectives: 17.5 us -> 99 us  [the longest x1 52.7 us: collect(): a = lax.all_to_all(a, 'tp', split_axis=0, concat_axis=0, tiled=True)]
    all_to_all x5 -> x7, waiting for transfers between devices: 42.1 us -> 111 us  [the longest x1 44.2 us: collect(): a = lax.all_to_all(a, 'tp', split_axis=0, concat_axis=0, tiled=True)]
    pallas_call x0 -> x1, Pallas kernels: none -> 44 us  [gradients(): pl.pallas_call(grad_kernel, grid_spec=pltpu.PrefetchScalarGridSpec(num_sc...]
    all_gather x0 -> x1, blocking collectives: none -> 34.2 us  [per_device(): first = lax.all_gather(dqd, 'tp', axis=0, tiled=True)]
    ppermute x4 -> x0, waiting for transfers between devices: 32.7 us -> none  [passed_along(): return lax.ppermute(value, axis, pairs)]
    dynamic_update_slice x14 -> x0, local copies, waits for them, and re-layouts: 31.8 us -> none  [the longest x2 18.3 us: grad_pass(): lax.scan(grad_advance, jnp.zeros(q_rows.shape, jnp.float32), (key_steps,...]
  transfers between devices with their start and end apart: 12 -> 8, of which waited for: 8 -> 7; matrix products, arithmetic and copies ran while one was open for 10% -> 7% of each run, Pallas kernels for 0% -> 0%
where the time goes in v1:
time: 371 us; the launch traced here: 369 us
  blocking collectives  133 us (36%)
  waiting for transfers between devices  111 us (30%)
  Pallas kernels  44 us (12%)
  starting transfers between devices  33.4 us (9%)
  local copies, waits for them, and re-layouts  27.8 us (7%)
  between operations  14.2 us (4%)
  other arithmetic  5.04 us (1%)
    all_to_all x1, blocking collectives, collect(): a = lax.all_to_all(a, 'tp', split_axis=0, concat_axis=0, tiled=True)  52.7 us
    all_to_all x1, waiting for transfers between devices, collect(): a = lax.all_to_all(a, 'tp', split_axis=0, concat_axis=0, tiled=True)  44.2 us
    pallas_call x1, Pallas kernels, gradients(): pl.pallas_call(grad_kernel, grid_spec=pltpu.PrefetchScalarGridSpec(num_sc...  44 us
    all_to_all x1, blocking collectives, per_device(): back = lambda a: swap(a, split_axis=0, concat_axis=1)  34.3 us
    all_gather x1, blocking collectives, per_device(): first = lax.all_gather(dqd, 'tp', axis=0, tiled=True)  34.2 us
    all_to_all x1, waiting for transfers between devices, per_device(): o = swap(output_gradient, split_axis=1, concat_axis=0)  23.3 us
    all_to_all x1, waiting for transfers between devices, per_device(): q = swap(queries, split_axis=1, concat_axis=0)  20.7 us
    all_to_all x2, waiting for transfers between devices, spread(): lax.all_to_all(a, 'tp', split_axis=0, concat_axis=0, tiled=True)[:rows]  17.8 us
  transfers between devices with their start and end apart: 8, of which 7 were waited for; matrix products, arithmetic and copies ran while one was open for 7% of the time, Pallas kernels for 0%

profile of v1, /device:TPU:1, one launch (start us, length us, event | category | flops | bytes accessed | tf_op | source)
XLA Modules:
  0.0 368.7 jit_solution(6824406900891326178)
XLA Ops:
  7.2 0.0 copy-start.1
  7.2 0.0 all-gather.2.cloned.1.call-start
  7.2 1.2 copy_bitcast_fusion
  8.5 12.0 %all_to_all.147 = bf16[128,4,512]{2,0,1:T(8,128)(2,1)} all-to-all(bf16[128,4,512]{2,0,1:T(8,128)(2,1)S(1)} %pad_maximum_fusion), channel_id=1, replica_groups=mesh['ctx'=4,'tp'=8] {'ctx'}, dimensions={1} | all-to-all | bytes 1048576 | tf_op jit(solution)/shard_map/all_to_all | solution.py:229
  20.5 0.0 all-gather.2.cloned.1.call-update
  20.5 0.0 copy-done.1
  20.5 2.4 copy.31
  23.0 4.6 %all-to-all-start = ((bf16[128,4,2048]{0,2,1:T(8,128)(2,1)}), bf16[128,4,2048]{0,2,1:T(8,128)(2,1)S(1)}, u32[]{:S(2)}, u32[]{:S(2)}) async-start(bf16[128,4,2048]{0,2,1:T(8,128)(2,1)} %bitcast.56), calls=%async_computation | async-start | bytes 4194304 | tf_op jit(solution)/shard_map/all_to_all | solution.py:231
  27.6 4.1 %copy.33 = bf16[128,8192]{0,1:T(8,128)(2,1)} copy(bf16[128,8192]{1,0:T(8,128)(2,1)} %param.9) | data formatting | bytes 4194304 | tf_op args[3]
  31.7 20.7 %all-to-all-done = bf16[128,4,2048]{0,2,1:T(8,128)(2,1)S(1)} async-done(((bf16[128,4,2048]{0,2,1:T(8,128)(2,1)}), bf16[128,4,2048]{0,2,1:T(8,128)(2,1)S(1)}, u32[]{:S(2)}, u32[]{:S(2)}) %all-to-all-start) | async-done | bytes 2097184 | tf_op jit(solution)/shard_map/all_to_all | solution.py:231
  52.4 5.3 %all-to-all-start.1 = ((bf16[128,4,2048]{0,2,1:T(8,128)(2,1)}), bf16[128,4,2048]{0,2,1:T(8,128)(2,1)}, u32[]{:S(2)}, u32[]{:S(2)}) async-start(bf16[128,4,2048]{0,2,1:T(8,128)(2,1)} %bitcast.55), calls=%async_computation.1 | async-start | bytes 4194304 | tf_op jit(solution)/shard_map/all_to_all | solution.py:232
  57.8 0.4 copy.37
  58.2 1.1 all_to_all.117
  59.3 23.3 %all-to-all-done.1 = bf16[128,4,2048]{0,2,1:T(8,128)(2,1)} async-done(((bf16[128,4,2048]{0,2,1:T(8,128)(2,1)}), bf16[128,4,2048]{0,2,1:T(8,128)(2,1)}, u32[]{:S(2)}, u32[]{:S(2)}) %all-to-all-start.1) | async-done | bytes 2097184 | tf_op jit(solution)/shard_map/all_to_all | solution.py:232
  82.7 6.0 %all-to-all-start.3 = ((bf16[8,128,256]{2,1,0:T(8,128)(2,1)}), bf16[8,128,256]{2,1,0:T(8,128)(2,1)}, u32[]{:S(2)}, u32[]{:S(2)}) async-start(bf16[8,128,256]{2,1,0:T(8,128)(2,1)} %all_to_all.117), calls=%async_computation.3 | async-start | bytes 1048576 | tf_op jit(solution)/shard_map/all_to_all | solution.py:236
  88.7 0.0 copy-start.3
  88.7 0.0 copy-start.4
  88.7 1.1 slice.32
  89.8 0.4 copy.38
  90.2 1.1 all_to_all.119
  91.4 14.7 %all-to-all-done.3 = bf16[8,128,256]{2,1,0:T(8,128)(2,1)} async-done(((bf16[8,128,256]{2,1,0:T(8,128)(2,1)}), bf16[8,128,256]{2,1,0:T(8,128)(2,1)}, u32[]{:S(2)}, u32[]{:S(2)}) %all-to-all-start.3) | async-done | bytes 524320 | tf_op jit(solution)/shard_map/all_to_all | solution.py:236
  106.0 3.5 all-to-all-start.4
  109.5 0.0 copy-done.3
  109.5 0.1 reshape.77
  109.6 0.0 copy-done.4
  109.6 0.1 reshape.79
  109.7 0.1 constant_dynamic-slice_fusion
  109.8 0.1 copy.46
  109.9 0.6 reshape_reshape.3.live
  110.5 0.1 copy.45
  110.6 0.1 reshape.78
  110.7 0.5 compare_convert_fusion.keep
  111.2 0.6 fusion.2.table
  111.8 2.6 copy.32
  114.4 4.0 %copy.34 = bf16[4,128,2048]{2,1,0:T(8,128)(2,1)} copy(bf16[4,128,2048]{1,2,0:T(8,128)(2,1)} %bitcast.4) | data formatting | bytes 4194304 | tf_op jit(solution)/shard_map/all_to_all | solution.py:232
  118.4 1.5 slice_bitcast_fusion.1.qd_ref
  119.9 3.2 all-to-all-done.4
  123.0 0.6 slice_bitcast_fusion.od_ref
  123.6 0.0 all-gather.2.cloned.1.call-done.k_ref.v_ref
  123.6 44.0 %shard_map.85 = (bf16[512,2048]{1,0:T(8,128)(2,1)}, bf16[4096,256]{1,0:T(8,128)(2,1)}, bf16[4096,256]{1,0:T(8,128)(2,1)}, bf16[128,256]{1,0:T(8,128)(2,1)}) custom-call(s32[32]{0:T(128)} %fusion.2.table, s32[32]{0:T(128)} %reshape_reshape.3.live, s32[4]{0:T(128)} %compare_convert_fusion.keep, bf16[512,2048]{1,0:T(8,128)(2,1)} %bitcast.59, ...), custom_call_target="tpu_custom_call" | custom-call | flops 13421772800 | bytes 25165824 | tf_op jit(solution)/shard_map/pallas_call | solution.py:153
  167.6 0.0 copy-start
  167.6 34.2 %all_gather.7 = bf16[1024,256]{1,0:T(8,128)(2,1)S(1)} all-gather(bf16[128,256]{1,0:T(8,128)(2,1)} %get-tuple-element.8), channel_id=1, replica_groups=mesh['ctx'=4,'tp'=8] {'tp'}, dimensions={0}, use_global_device_ids=true | all-gather | bytes 589824 | tf_op jit(solution)/shard_map/all_gather | solution.py:240
  201.8 0.1 reshape.84
  201.9 0.6 copy.39
  202.5 0.0 copy-done
  202.6 0.2 fusion
  202.8 0.0 copy-start.2
  202.8 34.3 %all_to_all.148 = bf16[4,128,2048]{2,1,0:T(8,128)(2,1)} all-to-all(bf16[4,128,2048]{2,1,0:T(8,128)(2,1)S(1)} %bitcast.57), channel_id=1, replica_groups=mesh['ctx'=4,'tp'=8] {'ctx'}, dimensions={0} | all-to-all | bytes 4194304 | tf_op jit(solution)/shard_map/all_to_all | solution.py:243
  237.1 0.0 copy-done.2
  237.1 52.7 %all_to_all.149 = bf16[8,512,256]{2,1,0:T(8,128)(2,1)} all-to-all(bf16[8,512,256]{2,1,0:T(8,128)(2,1)S(1)} %bitcast.61), channel_id=1, replica_groups=mesh['ctx'=4,'tp'=8] {'tp'}, dimensions={0} | all-to-all | bytes 4194304 | tf_op jit(solution)/shard_map/all_to_all | solution.py:246
  289.7 3.9 %all-to-all-start.8 = ((bf16[8,512,256]{2,1,0:T(8,128)(2,1)}), bf16[8,512,256]{2,1,0:T(8,128)(2,1)S(1)}, u32[]{:S(2)}, u32[]{:S(2)}) async-start(bf16[8,512,256]{2,1,0:T(8,128)(2,1)} %bitcast.58), calls=%async_computation.8 | async-start | bytes 4194304 | tf_op jit(solution)/shard_map/all_to_all | solution.py:246
  293.6 2.6 reduce_sum.24
  296.3 44.2 %all-to-all-done.8 = bf16[8,512,256]{2,1,0:T(8,128)(2,1)S(1)} async-done(((bf16[8,512,256]{2,1,0:T(8,128)(2,1)}), bf16[8,512,256]{2,1,0:T(8,128)(2,1)S(1)}, u32[]{:S(2)}, u32[]{:S(2)}) %all-to-all-start.8) | async-done | bytes 2097184 | tf_op jit(solution)/shard_map/all_to_all | solution.py:246
  340.5 5.7 %all-to-all-start.7 = ((bf16[4,128,256]{2,1,0:T(8,128)(2,1)}), bf16[4,128,256]{2,1,0:T(8,128)(2,1)S(1)}, u32[]{:S(2)}, u32[]{:S(2)}) async-start(bf16[4,128,256]{2,1,0:T(8,128)(2,1)} %bitcast.18), calls=%async_computation.7 | async-start | bytes 524288 | tf_op jit(solution)/shard_map/all_to_all | solution.py:243
  346.2 1.0 reduce_sum.25
  347.3 4.1 %all-to-all-done.7 = bf16[4,128,256]{2,1,0:T(8,128)(2,1)S(1)} async-done(((bf16[4,128,256]{2,1,0:T(8,128)(2,1)}), bf16[4,128,256]{2,1,0:T(8,128)(2,1)S(1)}, u32[]{:S(2)}, u32[]{:S(2)}) %all-to-all-start.7) | async-done | bytes 262176 | tf_op jit(solution)/shard_map/all_to_all | solution.py:243
  351.4 4.2 %all-to-all-start.9 = ((bf16[4,128,256]{2,1,0:T(8,128)(2,1)}), bf16[4,128,256]{2,1,0:T(8,128)(2,1)S(1)}, u32[]{:S(2)}, u32[]{:S(2)}) async-start(bf16[4,128,256]{2,1,0:T(8,128)(2,1)} %bitcast.22), calls=%async_computation.9 | async-start | bytes 524288 | tf_op jit(solution)/shard_map/all_to_all | solution.py:243
  355.6 3.2 copy.49
  358.8 0.2 copy.41
  359.0 0.9 copy.43
  359.8 1.0 all-to-all-done.9
  360.8 0.2 copy.42
  361.0 0.9 copy.44
  (2 shorter events, 0.1 us)
Async XLA Ops:
  7.2 13.3 %copy-start.1 = (bf16[128,8192]{1,0:T(8,128)(2,1)S(1)}, bf16[128,8192]{1,0:T(8,128)(2,1)}, u32[]{:S(2)}) copy-start(bf16[128,8192]{1,0:T(8,128)(2,1)} %param.6) | copy-start | bytes 6291460
  7.2 116.5 %all-gather.2.cloned.1.call-start = ((), (), s32[]{:S(2)}) async-start(), calls=%async_computation.10 | async-start | bytes 4718592 | tf_op jit(solution)/shard_map/all_gather | solution.py:230
  23.0 29.4 %all-to-all-start = ((bf16[128,4,2048]{0,2,1:T(8,128)(2,1)}), bf16[128,4,2048]{0,2,1:T(8,128)(2,1)S(1)}, u32[]{:S(2)}, u32[]{:S(2)}) async-start(bf16[128,4,2048]{0,2,1:T(8,128)(2,1)} %bitcast.56), calls=%async_computation | async-start | bytes 4194304 | tf_op jit(solution)/shard_map/all_to_all | solution.py:231
  52.4 30.3 %all-to-all-start.1 = ((bf16[128,4,2048]{0,2,1:T(8,128)(2,1)}), bf16[128,4,2048]{0,2,1:T(8,128)(2,1)}, u32[]{:S(2)}, u32[]{:S(2)}) async-start(bf16[128,4,2048]{0,2,1:T(8,128)(2,1)} %bitcast.55), calls=%async_computation.1 | async-start | bytes 4194304 | tf_op jit(solution)/shard_map/all_to_all | solution.py:232
  82.7 23.4 %all-to-all-start.3 = ((bf16[8,128,256]{2,1,0:T(8,128)(2,1)}), bf16[8,128,256]{2,1,0:T(8,128)(2,1)}, u32[]{:S(2)}, u32[]{:S(2)}) async-start(bf16[8,128,256]{2,1,0:T(8,128)(2,1)} %all_to_all.117), calls=%async_computation.3 | async-start | bytes 1048576 | tf_op jit(solution)/shard_map/all_to_all | solution.py:236
  88.7 20.8 %copy-start.3 = (s32[32,8]{0,1:T(8,128)S(1)}, s32[32,8]{0,1:T(8,128)}, u32[]{:S(2)}) copy-start(s32[32,8]{0,1:T(8,128)} %param.10) | copy-start | bytes 3076
  88.7 20.9 %copy-start.4 = (s32[32,8]{0,1:T(8,128)S(1)}, s32[32,8]{0,1:T(8,128)}, u32[]{:S(2)}) copy-start(s32[32,8]{0,1:T(8,128)} %param.11) | copy-start | bytes 3076
  106.0 17.0 %all-to-all-start.4 = ((bf16[8,128,256]{2,1,0:T(8,128)(2,1)}), bf16[8,128,256]{2,1,0:T(8,128)(2,1)S(1)}, u32[]{:S(2)}, u32[]{:S(2)}) async-start(bf16[8,128,256]{2,1,0:T(8,128)(2,1)} %all_to_all.119), calls=%async_computation.4 | async-start | bytes 1048576 | tf_op jit(solution)/shard_map/all_to_all | solution.py:236
  167.6 34.9 %copy-start = (bf16[512,2048]{1,0:T(8,128)(2,1)S(1)}, bf16[512,2048]{1,0:T(8,128)(2,1)}, u32[]{:S(2)}) copy-start(bf16[512,2048]{1,0:T(8,128)(2,1)} %get-tuple-element.7) | copy-start | bytes 6291460
  202.8 34.3 %copy-start.2 = (bf16[4096,256]{1,0:T(8,128)(2,1)S(1)}, bf16[4096,256]{1,0:T(8,128)(2,1)}, u32[]{:S(2)}) copy-start(bf16[4096,256]{1,0:T(8,128)(2,1)} %get-tuple-element.9) | copy-start | bytes 6291460
  289.7 50.8 %all-to-all-start.8 = ((bf16[8,512,256]{2,1,0:T(8,128)(2,1)}), bf16[8,512,256]{2,1,0:T(8,128)(2,1)S(1)}, u32[]{:S(2)}, u32[]{:S(2)}) async-start(bf16[8,512,256]{2,1,0:T(8,128)(2,1)} %bitcast.58), calls=%async_computation.8 | async-start | bytes 4194304 | tf_op jit(solution)/shard_map/all_to_all | solution.py:246
  340.5 10.9 %all-to-all-start.7 = ((bf16[4,128,256]{2,1,0:T(8,128)(2,1)}), bf16[4,128,256]{2,1,0:T(8,128)(2,1)S(1)}, u32[]{:S(2)}, u32[]{:S(2)}) async-start(bf16[4,128,256]{2,1,0:T(8,128)(2,1)} %bitcast.18), calls=%async_computation.7 | async-start | bytes 524288 | tf_op jit(solution)/shard_map/all_to_all | solution.py:243
  351.4 9.4 %all-to-all-start.9 = ((bf16[4,128,256]{2,1,0:T(8,128)(2,1)}), bf16[4,128,256]{2,1,0:T(8,128)(2,1)S(1)}, u32[]{:S(2)}, u32[]{:S(2)}) async-start(bf16[4,128,256]{2,1,0:T(8,128)(2,1)} %bitcast.22), calls=%async_computation.9 | async-start | bytes 524288 | tf_op jit(solution)/shard_map/all_to_all | solution.py:243
Sparse Core Ops, SparseCore 0:
  20.6 73.5 all-gather.1

commit v2 on v1

--- a/solution.py
+++ b/solution.py
@@ -13,6 +13,7 @@
 BLOCK_TOKENS = 128
 NB = 8
 GROUP_SIZE = 8
+SUB = 2
 
 SCALE = 1.0 / math.sqrt(HEAD_SIZE)
 LOG_SCALE = SCALE * math.log2(math.e)
@@ -213,6 +214,219 @@
     return place.astype(jnp.int32), pick(slot_valid), (own != 0).astype(jnp.int32)
 
 
+def ring_place(t, n):
+    odd = t % 2
+    return (1 - odd) * (t // 2) + odd * (n - 1 - t // 2)
+
+
+def ring_owner(p, n):
+    p = (p + 2 * n) % n
+    far = p // (n // 2)
+    return (1 - far) * 2 * p + far * (2 * (n - 1 - p) + 1)
+
+
+def signal(sem, c, t):
+    pl.semaphore_signal(sem, inc=1, device_id=(c, t), device_id_type=pl.DeviceIdType.MESH)
+
+
+def meet(c, t, ctx, tp, before, after):
+    barrier = pltpu.get_barrier_semaphore()
+    for k in range(1, ctx):
+        signal(barrier, (c + k) % ctx, t)
+    signal(barrier, c, before)
+    signal(barrier, c, after)
+    origin = c * tp + t == 0
+
+    @pl.when(origin)
+    def greet():
+        def one(i, none):
+            signal(barrier, i // tp, i % tp)
+            return none
+
+        lax.fori_loop(1, ctx * tp, one, 0)
+        pl.semaphore_wait(barrier, ctx + 1 + ctx * tp - 1)
+
+    @pl.when(jnp.logical_not(origin))
+    def answer():
+        signal(barrier, 0, 0)
+        pl.semaphore_wait(barrier, ctx + 2)
+
+    return origin
+
+
+def remote(src, dst, send, recv, c, t):
+    return pltpu.make_async_remote_copy(
+        src_ref=src, dst_ref=dst, send_sem=send, recv_sem=recv,
+        device_id=(c, t), device_id_type=pl.DeviceIdType.MESH,
+    )
+
+
+def await_bytes(ref, sem):
+    pltpu.make_async_copy(ref, ref, sem).wait()
+
+
+def return_kernel(
+    ctx, tp,
+    dq_ref, dqd_ref, dk_ref, dv_ref,
+    dq_out, dk_out, dv_out,
+    got, done, ring_send, ring_recv, q_send, q_recv, d_send, g_send, g_recv,
+):
+    c = lax.axis_index("ctx")
+    t = lax.axis_index("tp")
+    tokens = dq_out.shape[0]
+    width = dq_ref.shape[1]
+    thin = dk_ref.shape[1]
+    heads = thin // D
+    chunk = ctx * tokens
+    part = chunk // SUB
+    p = ring_place(t, tp)
+    after = ring_owner(p + 1, tp)
+    before = ring_owner(p - 1, tp)
+    origin = meet(c, t, ctx, tp, before, after)
+    ways = ((dk_ref, 1, after), (dv_ref, -1, before))
+
+    def own(way, place, sub):
+        at = pl.multiple_of(ring_owner(place, tp) * chunk + sub * part, part)
+        return ways[way][0].at[pl.ds(at, part), :]
+
+    def hop(way, src, step, sub):
+        return remote(
+            src, got.at[way, step, sub], ring_send.at[way, step, sub],
+            ring_recv.at[way, step, sub], c, ways[way][2],
+        )
+
+    for sub in range(SUB):
+        for way in range(2):
+            hop(way, own(way, p - ways[way][1], sub), 0, sub).start()
+
+    def rows_of(k):
+        return dq_ref.at[pl.ds(pl.multiple_of(k * tokens, tokens), tokens), :]
+
+    columns = dq_out.at[:, pl.ds(pl.multiple_of(c * width, width), width)]
+    for k in range(1, ctx):
+        peer = (c + k) % ctx
+
+        @pl.when(peer * tp + t != 0)
+        def send():
+            remote(rows_of(peer), columns, q_send.at[k], q_recv, peer, t).start()
+
+    @pl.when(jnp.logical_not(origin))
+    def keep_rows():
+        pltpu.make_async_copy(rows_of(c), columns, q_recv).start()
+
+    rows = dqd_ref.shape[0]
+    first = t * rows
+    token = pl.multiple_of(first % T, rows)
+
+    def dense(h):
+        column = c * width + h * (GROUP_SIZE * D) + (first // T) * D
+        return (
+            dqd_ref.at[:, h * D:(h + 1) * D],
+            dq_out.at[pl.ds(token, rows), pl.ds(pl.multiple_of(column, D), D)],
+        )
+
+    for h in range(heads):
+        src, dst = dense(h)
+
+        @pl.when(origin)
+        def stay():
+            pltpu.make_async_copy(src, dst, q_recv).start()
+
+        @pl.when(jnp.logical_not(origin))
+        def leave():
+            remote(src, dst, d_send.at[h], q_recv, 0, 0).start()
+
+    def total(way, step, sub):
+        hop(way, got.at[way, step, sub], step, sub).wait_recv()
+        place = p - ways[way][1] * (step + 2)
+        return got[way, step, sub].astype(F32) + own(way, place, sub)[...].astype(F32)
+
+    def advance(step, none):
+        for sub in range(SUB):
+            for way in range(2):
+                got[way, step - 1, sub] = total(way, step - 1, sub).astype(BF16)
+                hop(way, got.at[way, step - 1, sub], step, sub).start()
+        return none
+
+    lax.fori_loop(1, tp - 1, advance, 0)
+    outs = (dk_out, dv_out)
+
+    def give(way, peer, k):
+        src = done.at[way, pl.ds(pl.multiple_of(peer * tokens, tokens), tokens), :]
+        dst = outs[way].at[:, pl.ds(pl.multiple_of(c * thin, thin), thin)]
+        return src, dst
+
+    for sub in range(SUB):
+        for way in range(2):
+            done[way, sub * part:(sub + 1) * part, :] = total(way, tp - 2, sub).astype(BF16)
+    for way in range(2):
+        for k in range(1, ctx):
+            peer = (c + k) % ctx
+            src, dst = give(way, peer, k)
+            remote(src, dst, g_send.at[way, k], g_recv.at[way], peer, t).start()
+        src, dst = give(way, c, 0)
+        pltpu.make_async_copy(src, dst, g_recv.at[way]).start()
+
+    await_bytes(dq_out, q_recv)
+    for way in range(2):
+        await_bytes(outs[way], g_recv.at[way])
+    for way in range(2):
+        for k in range(1, ctx):
+            peer = (c + k) % ctx
+            src, dst = give(way, peer, k)
+            remote(src, dst, g_send.at[way, k], g_recv.at[way], peer, t).wait_send()
+    for k in range(1, ctx):
+        peer = (c + k) % ctx
+
+        @pl.when(peer * tp + t != 0)
+        def sent():
+            remote(rows_of(peer), columns, q_send.at[k], q_recv, peer, t).wait_send()
+
+    for h in range(heads):
+        src, dst = dense(h)
+
+        @pl.when(jnp.logical_not(origin))
+        def left():
+            remote(src, dst, d_send.at[h], q_recv, 0, 0).wait_send()
+
+    def settle(step, none):
+        for sub in range(SUB):
+            for way in range(2):
+                hop(way, got.at[way, step, sub], step, sub).wait_send()
+        return none
+
+    lax.fori_loop(0, tp - 1, settle, 0)
+
+
+def send_back(dq, dqd, dk, dv, ctx, tp):
+    tokens = dq.shape[0] // ctx
+    thin = dk.shape[1]
+    heads = thin // D
+    part = ctx * tokens // SUB
+    anywhere = pl.BlockSpec(memory_space=pl.ANY)
+    vmem = pl.BlockSpec(memory_space=pltpu.VMEM)
+    dma = pltpu.SemaphoreType.DMA
+    return pl.pallas_call(
+        functools.partial(return_kernel, ctx, tp),
+        in_specs=[anywhere, anywhere, vmem, vmem],
+        out_specs=[anywhere, anywhere, anywhere],
+        out_shape=[
+            jax.ShapeDtypeStruct((tokens, ctx * dq.shape[1]), BF16),
+            jax.ShapeDtypeStruct((tokens, ctx * thin), BF16),
+            jax.ShapeDtypeStruct((tokens, ctx * thin), BF16),
+        ],
+        scratch_shapes=[
+            pltpu.VMEM((2, tp - 1, SUB, part, thin), BF16),
+            pltpu.VMEM((2, ctx * tokens, thin), BF16),
+            dma((2, tp - 1, SUB)), dma((2, tp - 1, SUB)),
+            dma((ctx,)), dma, dma((heads,)), dma((2, ctx)), dma((2,)),
+        ],
+        compiler_params=pltpu.CompilerParams(
+            collective_id=1, has_side_effects=True, vmem_limit_bytes=48 * 1024 * 1024
+        ),
+    )(dq, dqd, dk, dv)
+
+
 def per_device(queries, key_tensor, value_tensor, output_gradient, key_blocks, slot_valid):
     ctx = lax.axis_size("ctx")
     tp = lax.axis_size("tp")
@@ -220,8 +434,6 @@
     pieces = tokens // T
     heads = KEY_HEADS // ctx
     rows = GROUP_SIZE * T // tp
-    wide = GROUP_SIZE * D
-    tp_index = lax.axis_index("tp")
     swap = functools.partial(lax.all_to_all, axis_name="ctx", tiled=True)
     kv = jnp.concatenate(
         [key_tensor.reshape(tokens, ctx, heads * D), value_tensor.reshape(tokens, ctx, heads * D)], axis=2
@@ -237,16 +449,7 @@
 
     table, live, keep = tables(key_blocks, slot_valid, ctx, tp, pieces)
     dq, dk, dv, dqd = gradients(table, live, keep, q, o, kv, spread(q), spread(o))
-    first = lax.all_gather(dqd, "tp", axis=0, tiled=True)
-    first = first.reshape(GROUP_SIZE, T, heads, D).transpose(1, 2, 0, 3).reshape(T, heads * wide)
-    dq = lax.dynamic_update_slice(dq, jnp.where(tp_index == 0, first, dq[:T]), (0, 0))
-    back = lambda a: swap(a, split_axis=0, concat_axis=1)
-
-    def collect(a):
-        a = lax.all_to_all(a, "tp", split_axis=0, concat_axis=0, tiled=True)
-        return jnp.sum(a.reshape(tp, ctx * tokens, heads * D).astype(F32), axis=0).astype(BF16)
-
-    return back(dq), back(collect(dk)), back(collect(dv))
+    return tuple(send_back(dq, dqd, dk, dv, ctx, tp))
 
 
 def solution(mesh):

time: 371 us -> 251 us (0.68)
  blocking collectives: 133 us -> 12 us
  Pallas kernels: 44 us -> 115 us
  waiting for transfers between devices: 111 us -> 61.9 us
  starting transfers between devices: 33.4 us -> 19.5 us
  other arithmetic: 5.04 us -> 1.13 us
    all_to_all x2 -> x0, blocking collectives: 86.9 us -> none  [the longest x1 52.7 us: collect(): a = lax.all_to_all(a, 'tp', split_axis=0, concat_axis=0, tiled=True)]
    pallas_call x0 -> x1, Pallas kernels: none -> 71 us  [send_back(): pl.pallas_call(functools.partial(return_kernel, ctx, tp), in_specs=[anywh...]
    all_to_all x3 -> x0, waiting for transfers between devices: 49.3 us -> none  [the longest x1 44.2 us: collect(): a = lax.all_to_all(a, 'tp', split_axis=0, concat_axis=0, tiled=True)]
    all_gather x1 -> x0, blocking collectives: 34.2 us -> none  [per_device(): first = lax.all_gather(dqd, 'tp', axis=0, tiled=True)]
    all_to_all x3 -> x0, starting transfers between devices: 13.9 us -> none  [the longest x2 9.97 us: per_device(): back = lambda a: swap(a, split_axis=0, concat_axis=1)]
    unnamed x16 -> x17, local copies, waits for them, and re-layouts: 8.49 us -> 11.9 us
  transfers between devices with their start and end apart: 8 -> 5, of which waited for: 7 -> 4; matrix products, arithmetic and copies ran while one was open for 7% -> 8% of each run, Pallas kernels for 0% -> 0%
where the time goes in v2:
time: 251 us
  Pallas kernels  115 us (46%)
  waiting for transfers between devices  61.9 us (25%)
  local copies, waits for them, and re-layouts  27 us (11%)
  starting transfers between devices  19.5 us (8%)
  between operations  14.1 us (6%)
  blocking collectives  12 us (5%)
    pallas_call x1, Pallas kernels, send_back(): pl.pallas_call(functools.partial(return_kernel, ctx, tp), in_specs=[anywh...  71 us
    pallas_call x1, Pallas kernels, gradients(): pl.pallas_call(grad_kernel, grid_spec=pltpu.PrefetchScalarGridSpec(num_sc...  43.9 us
    all_to_all x1, waiting for transfers between devices, per_device(): o = swap(output_gradient, split_axis=1, concat_axis=0)  23.3 us
    all_to_all x1, waiting for transfers between devices, per_device(): q = swap(queries, split_axis=1, concat_axis=0)  20.7 us
    all_to_all x2, waiting for transfers between devices, spread(): lax.all_to_all(a, 'tp', split_axis=0, concat_axis=0, tiled=True)[:rows]  17.8 us
    all_to_all x1, blocking collectives, per_device(): kv = swap(kv, split_axis=1, concat_axis=0)  12 us
    unnamed x17, local copies, waits for them, and re-layouts  11.9 us
    all_to_all x2, starting transfers between devices, spread(): lax.all_to_all(a, 'tp', split_axis=0, concat_axis=0, tiled=True)[:rows]  9.51 us
  transfers between devices with their start and end apart: 5, of which 4 were waited for; matrix products, arithmetic and copies ran while one was open for 8% of the time, Pallas kernels for 0%

profile of v2, /device:TPU:1, one launch (start us, length us, event | category | flops | bytes accessed | tf_op | source)
XLA Modules:
  0.0 250.5 jit_solution(3819570344387473516)
XLA Ops:
  7.2 0.0 copy-start.2
  7.2 0.0 all-gather.2.cloned.1.call-start
  7.2 1.2 copy_bitcast_fusion
  8.5 12.0 %all_to_all.72 = bf16[128,4,512]{2,0,1:T(8,128)(2,1)} all-to-all(bf16[128,4,512]{2,0,1:T(8,128)(2,1)S(1)} %pad_maximum_fusion), channel_id=1, replica_groups=mesh['ctx'=4,'tp'=8] {'ctx'}, dimensions={1} | all-to-all | bytes 1048576 | tf_op jit(solution)/shard_map/all_to_all | solution.py:441
  20.5 0.0 all-gather.2.cloned.1.call-update
  20.5 0.0 copy-done.2
  20.5 2.4 copy.17
  23.0 4.6 %all-to-all-start = ((bf16[128,4,2048]{0,2,1:T(8,128)(2,1)}), bf16[128,4,2048]{0,2,1:T(8,128)(2,1)S(1)}, u32[]{:S(2)}, u32[]{:S(2)}) async-start(bf16[128,4,2048]{0,2,1:T(8,128)(2,1)} %bitcast.36), calls=%async_computation | async-start | bytes 4194304 | tf_op jit(solution)/shard_map/all_to_all | solution.py:443
  27.6 4.1 %copy.19 = bf16[128,8192]{0,1:T(8,128)(2,1)} copy(bf16[128,8192]{1,0:T(8,128)(2,1)} %param.9) | data formatting | bytes 4194304 | tf_op args[3]
  31.7 20.7 %all-to-all-done = bf16[128,4,2048]{0,2,1:T(8,128)(2,1)S(1)} async-done(((bf16[128,4,2048]{0,2,1:T(8,128)(2,1)}), bf16[128,4,2048]{0,2,1:T(8,128)(2,1)S(1)}, u32[]{:S(2)}, u32[]{:S(2)}) %all-to-all-start) | async-done | bytes 2097184 | tf_op jit(solution)/shard_map/all_to_all | solution.py:443
  52.4 5.3 %all-to-all-start.1 = ((bf16[128,4,2048]{0,2,1:T(8,128)(2,1)}), bf16[128,4,2048]{0,2,1:T(8,128)(2,1)}, u32[]{:S(2)}, u32[]{:S(2)}) async-start(bf16[128,4,2048]{0,2,1:T(8,128)(2,1)} %bitcast.35), calls=%async_computation.1 | async-start | bytes 4194304 | tf_op jit(solution)/shard_map/all_to_all | solution.py:444
  57.8 0.4 copy.23
  58.2 1.1 all_to_all.63
  59.3 23.3 %all-to-all-done.1 = bf16[128,4,2048]{0,2,1:T(8,128)(2,1)} async-done(((bf16[128,4,2048]{0,2,1:T(8,128)(2,1)}), bf16[128,4,2048]{0,2,1:T(8,128)(2,1)}, u32[]{:S(2)}, u32[]{:S(2)}) %all-to-all-start.1) | async-done | bytes 2097184 | tf_op jit(solution)/shard_map/all_to_all | solution.py:444
  82.7 6.0 %all-to-all-start.3 = ((bf16[8,128,256]{2,1,0:T(8,128)(2,1)}), bf16[8,128,256]{2,1,0:T(8,128)(2,1)}, u32[]{:S(2)}, u32[]{:S(2)}) async-start(bf16[8,128,256]{2,1,0:T(8,128)(2,1)} %all_to_all.63), calls=%async_computation.3 | async-start | bytes 1048576 | tf_op jit(solution)/shard_map/all_to_all | solution.py:448
  88.7 0.0 copy-start.3
  88.7 0.0 copy-start.4
  88.7 1.1 slice.28
  89.8 0.4 copy.24
  90.2 1.1 all_to_all.65
  91.4 14.7 %all-to-all-done.3 = bf16[8,128,256]{2,1,0:T(8,128)(2,1)} async-done(((bf16[8,128,256]{2,1,0:T(8,128)(2,1)}), bf16[8,128,256]{2,1,0:T(8,128)(2,1)}, u32[]{:S(2)}, u32[]{:S(2)}) %all-to-all-start.3) | async-done | bytes 524320 | tf_op jit(solution)/shard_map/all_to_all | solution.py:448
  106.0 3.5 %all-to-all-start.4 = ((bf16[8,128,256]{2,1,0:T(8,128)(2,1)}), bf16[8,128,256]{2,1,0:T(8,128)(2,1)S(1)}, u32[]{:S(2)}, u32[]{:S(2)}) async-start(bf16[8,128,256]{2,1,0:T(8,128)(2,1)} %all_to_all.65), calls=%async_computation.4 | async-start | bytes 1048576 | tf_op jit(solution)/shard_map/all_to_all | solution.py:448
  109.5 0.0 copy-done.3
  109.5 0.1 reshape.54
  109.6 0.0 copy-done.4
  109.6 0.1 reshape.56
  109.7 0.1 constant_dynamic-slice_fusion
  109.8 0.1 copy.26
  109.9 0.6 reshape_reshape.3.live
  110.5 0.1 copy.25
  110.6 0.1 reshape.55
  110.7 0.5 compare_convert_fusion.keep
  111.2 0.6 fusion.1.table
  111.8 2.6 %copy.18 = bf16[4,128,2048]{2,1,0:T(8,128)(2,1)} copy(bf16[4,128,2048]{1,2,0:T(8,128)(2,1)S(1)} %bitcast.34) | data formatting | bytes 4194304 | tf_op jit(solution)/shard_map/all_to_all | solution.py:443
  114.4 4.0 %copy.20 = bf16[4,128,2048]{2,1,0:T(8,128)(2,1)} copy(bf16[4,128,2048]{1,2,0:T(8,128)(2,1)} %bitcast.4) | data formatting | bytes 4194304 | tf_op jit(solution)/shard_map/all_to_all | solution.py:444
  118.4 1.5 slice_bitcast_fusion.1.qd_ref
  119.9 3.2 %all-to-all-done.4 = bf16[8,128,256]{2,1,0:T(8,128)(2,1)S(1)} async-done(((bf16[8,128,256]{2,1,0:T(8,128)(2,1)}), bf16[8,128,256]{2,1,0:T(8,128)(2,1)S(1)}, u32[]{:S(2)}, u32[]{:S(2)}) %all-to-all-start.4) | async-done | bytes 524320 | tf_op jit(solution)/shard_map/all_to_all | solution.py:448
  123.0 0.6 slice_bitcast_fusion.od_ref
  123.6 0.0 all-gather.2.cloned.1.call-done.k_ref.v_ref
  123.6 43.9 %shard_map.85 = (bf16[512,2048]{1,0:T(8,128)(2,1)}, bf16[4096,256]{1,0:T(8,128)(2,1)}, bf16[4096,256]{1,0:T(8,128)(2,1)}, bf16[128,256]{1,0:T(8,128)(2,1)}) custom-call(s32[32]{0:T(128)} %fusion.1.table, s32[32]{0:T(128)} %reshape_reshape.3.live, s32[4]{0:T(128)} %compare_convert_fusion.keep, bf16[512,2048]{1,0:T(8,128)(2,1)} %bitcast.37, ...), custom_call_target="tpu_custom_call" | custom-call | flops 13421772800 | bytes 25165824 | tf_op jit(solution)/shard_map/pallas_call | solution.py:154
  167.5 0.0 copy-start
  167.5 1.6 copy-done
  169.1 0.0 copy-start.1
  169.1 0.8 copy-done.1
  170.0 71.0 %shard_map.86 = (bf16[128,8192]{1,0:T(8,128)(2,1)S(1)}, bf16[128,1024]{1,0:T(8,128)(2,1)S(1)}, bf16[128,1024]{1,0:T(8,128)(2,1)S(1)}) custom-call(bf16[512,2048]{1,0:T(8,128)(2,1)S(1)} %copy-done, bf16[128,256]{1,0:T(8,128)(2,1)S(1)} %copy-done.1, bf16[4096,256]{1,0:T(8,128)(2,1)} %get-tuple-element.9.dk_ref, bf16[4096,256]{1,0:T(8,128)(2,1)} %get-tuple-element.10.dv_ref), custom_call_target="tpu_custom_call" | custom-call | tf_op jit(solution)/shard_map/pallas_call | solution.py:409
  240.9 1.3 copy.34
  242.3 0.7 copy.35
  243.0 0.7 copy.36
  (2 shorter events, 0.1 us)
Async XLA Ops:
  7.2 13.3 %copy-start.2 = (bf16[128,8192]{1,0:T(8,128)(2,1)S(1)}, bf16[128,8192]{1,0:T(8,128)(2,1)}, u32[]{:S(2)}) copy-start(bf16[128,8192]{1,0:T(8,128)(2,1)} %param.6) | copy-start | bytes 6291460
  7.2 116.5 %all-gather.2.cloned.1.call-start = ((), (), s32[]{:S(2)}) async-start(), calls=%async_computation.5 | async-start | bytes 4718592 | tf_op jit(solution)/shard_map/all_gather | solution.py:442
  23.0 29.4 %all-to-all-start = ((bf16[128,4,2048]{0,2,1:T(8,128)(2,1)}), bf16[128,4,2048]{0,2,1:T(8,128)(2,1)S(1)}, u32[]{:S(2)}, u32[]{:S(2)}) async-start(bf16[128,4,2048]{0,2,1:T(8,128)(2,1)} %bitcast.36), calls=%async_computation | async-start | bytes 4194304 | tf_op jit(solution)/shard_map/all_to_all | solution.py:443
  52.4 30.3 %all-to-all-start.1 = ((bf16[128,4,2048]{0,2,1:T(8,128)(2,1)}), bf16[128,4,2048]{0,2,1:T(8,128)(2,1)}, u32[]{:S(2)}, u32[]{:S(2)}) async-start(bf16[128,4,2048]{0,2,1:T(8,128)(2,1)} %bitcast.35), calls=%async_computation.1 | async-start | bytes 4194304 | tf_op jit(solution)/shard_map/all_to_all | solution.py:444
  82.7 23.4 %all-to-all-start.3 = ((bf16[8,128,256]{2,1,0:T(8,128)(2,1)}), bf16[8,128,256]{2,1,0:T(8,128)(2,1)}, u32[]{:S(2)}, u32[]{:S(2)}) async-start(bf16[8,128,256]{2,1,0:T(8,128)(2,1)} %all_to_all.63), calls=%async_computation.3 | async-start | bytes 1048576 | tf_op jit(solution)/shard_map/all_to_all | solution.py:448
  88.7 20.8 %copy-start.3 = (s32[32,8]{0,1:T(8,128)S(1)}, s32[32,8]{0,1:T(8,128)}, u32[]{:S(2)}) copy-start(s32[32,8]{0,1:T(8,128)} %param.10) | copy-start | bytes 3076
  88.7 20.9 %copy-start.4 = (s32[32,8]{0,1:T(8,128)S(1)}, s32[32,8]{0,1:T(8,128)}, u32[]{:S(2)}) copy-start(s32[32,8]{0,1:T(8,128)} %param.11) | copy-start | bytes 3076
  106.0 17.0 %all-to-all-start.4 = ((bf16[8,128,256]{2,1,0:T(8,128)(2,1)}), bf16[8,128,256]{2,1,0:T(8,128)(2,1)S(1)}, u32[]{:S(2)}, u32[]{:S(2)}) async-start(bf16[8,128,256]{2,1,0:T(8,128)(2,1)} %all_to_all.65), calls=%async_computation.4 | async-start | bytes 1048576 | tf_op jit(solution)/shard_map/all_to_all | solution.py:448
  167.5 1.6 copy-start
  169.1 0.8 copy-start.1
Sparse Core Ops, SparseCore 0:
  20.6 73.5 all-gather.1

commit v3 on v2

--- a/solution.py
+++ b/solution.py
@@ -140,10 +140,10 @@
         dv_ref[...] = acc_v[...].astype(BF16)
 
 
-def gradients(table, live, keep, q, o, kv, qd, od):
+def gradients(table, live, keep, q, o, k, v, qd, od):
     blocks = table.shape[0]
-    length = kv.shape[0]
-    heads = kv.shape[1] // (2 * D)
+    length = k.shape[0]
+    heads = k.shape[1] // D
     rows = qd.shape[0]
     wide = GROUP_SIZE * D
     spec = lambda shape, index: pl.BlockSpec(shape, index)
@@ -159,7 +159,7 @@
             in_specs=[
                 row_block, row_block,
                 fixed(lambda h, j, *_: (0, h)),
-                fixed(lambda h, j, *_: (0, heads + h)),
+                fixed(lambda h, j, *_: (0, h)),
                 dense, dense,
             ],
             out_specs=[
@@ -195,10 +195,10 @@
         ),
         cost_estimate=pl.CostEstimate(
             flops=10 * heads * (blocks + 1) * (wide * NB * T * D),
-            bytes_accessed=4 * q.size * 2 + 4 * kv.size * 2,
+            bytes_accessed=6 * q.size + 8 * k.size,
             transcendentals=heads * (blocks + 1) * wide * NB * T,
         ),
-    )(table.reshape(-1), live.reshape(-1), keep, q, o, kv, kv, qd, od)
+    )(table.reshape(-1), live.reshape(-1), keep, q, o, k, v, qd, od)
 
 
 def tables(key_blocks, slot_valid, ctx, tp, pieces):
@@ -427,28 +427,191 @@
     )(dq, dqd, dk, dv)
 
 
+def exchange_kernel(
+    ctx, tp,
+    q_ref, o_ref, k_ref, v_ref,
+    q_out, o_out, k_out, v_out, qd_out, od_out,
+    kv_send, kv_recv, ring_send, ring_recv, qo_send, qo_recv, d_send, d_recv,
+):
+    c = lax.axis_index("ctx")
+    t = lax.axis_index("tp")
+    tokens = q_ref.shape[0]
+    width = q_out.shape[1]
+    thin = k_out.shape[1]
+    heads = thin // D
+    chunk = ctx * tokens
+    part = chunk // SUB
+    p = ring_place(t, tp)
+    after = ring_owner(p + 1, tp)
+    before = ring_owner(p - 1, tp)
+    origin = meet(c, t, ctx, tp, before, after)
+    thins = ((k_ref, k_out), (v_ref, v_out))
+    wides = ((q_ref, q_out), (o_ref, o_out))
+    mine = pl.multiple_of(t * chunk + c * tokens, tokens)
+
+    def thin_copy(way, peer):
+        src, dst = thins[way]
+        return src.at[:, pl.ds(pl.multiple_of(peer * thin, thin), thin)], dst.at[pl.ds(mine, tokens), :]
+
+    for k in range(1, ctx):
+        peer = (c + k) % ctx
+        for way in range(2):
+            src, dst = thin_copy(way, peer)
+            remote(src, dst, kv_send.at[way, k], kv_recv.at[way], peer, t).start()
+    for way in range(2):
+        src, dst = thin_copy(way, c)
+        pltpu.make_async_copy(src, dst, kv_recv.at[way]).start()
+
+    def wide_copy(i, peer):
+        src, dst = wides[i]
+        return (
+            src.at[:, pl.ds(pl.multiple_of(peer * width, width), width)],
+            dst.at[pl.ds(pl.multiple_of(c * tokens, tokens), tokens), :],
+        )
+
+    @pl.when(jnp.logical_not(origin))
+    def wide_start():
+        for i in range(2):
+            for k in range(1, ctx):
+                peer = (c + k) % ctx
+                src, dst = wide_copy(i, peer)
+                remote(src, dst, qo_send.at[i, k], qo_recv.at[i], peer, t).start()
+            src, dst = wide_copy(i, c)
+            pltpu.make_async_copy(src, dst, qo_recv.at[i]).start()
+
+    rows = qd_out.shape[0]
+    dense_outs = (qd_out, od_out)
+
+    def dense(i, h, c_to, t_to):
+        first = t_to * rows
+        column = c_to * width + h * (GROUP_SIZE * D) + (first // T) * D
+        return (
+            wides[i][0].at[
+                pl.ds(pl.multiple_of(first % T, rows), rows), pl.ds(pl.multiple_of(column, D), D)
+            ],
+            dense_outs[i].at[:, h * D:(h + 1) * D],
+        )
+
+    @pl.when(origin)
+    def dense_start():
+        def one(n, none):
+            for i in range(2):
+                for h in range(heads):
+                    src, dst = dense(i, h, n // tp, n % tp)
+                    remote(src, dst, d_send.at[i], d_recv.at[i], n // tp, n % tp).start()
+            return none
+
+        lax.fori_loop(1, ctx * tp, one, 0)
+        for i in range(2):
+            for h in range(heads):
+                src, dst = dense(i, h, 0, 0)
+                pltpu.make_async_copy(src, dst, d_recv.at[i]).start()
+
+    def hop(way, step, sub):
+        place = p - step if way == 0 else p + step
+        at = pl.multiple_of(ring_owner(place, tp) * chunk + sub * part, part)
+        ref = thins[way][1].at[pl.ds(at, part), :]
+        return remote(
+            ref, ref, ring_send.at[way, step, sub], ring_recv.at[way, step, sub],
+            c, (after, before)[way],
+        )
+
+    for way in range(2):
+        at = pl.multiple_of(t * chunk, chunk)
+        await_bytes(thins[way][1].at[pl.ds(at, chunk), :], kv_recv.at[way])
+        for sub in range(SUB):
+            hop(way, 0, sub).start()
+
+    def advance(step, none):
+        for sub in range(SUB):
+            for way in range(2):
+                hop(way, step - 1, sub).wait_recv()
+                hop(way, step, sub).start()
+        return none
+
+    lax.fori_loop(1, tp - 1, advance, 0)
+    for sub in range(SUB):
+        for way in range(2):
+            hop(way, tp - 2, sub).wait_recv()
+
+    for i in range(2):
+        await_bytes(dense_outs[i], d_recv.at[i])
+
+        @pl.when(t == 0)
+        def part_rows():
+            await_bytes(wides[i][1].at[tokens:, :], qo_recv.at[i])
+
+        @pl.when(t != 0)
+        def all_rows():
+            await_bytes(wides[i][1], qo_recv.at[i])
+
+    for way in range(2):
+        for k in range(1, ctx):
+            peer = (c + k) % ctx
+            src, dst = thin_copy(way, peer)
+            remote(src, dst, kv_send.at[way, k], kv_recv.at[way], peer, t).wait_send()
+
+    @pl.when(jnp.logical_not(origin))
+    def wide_sent():
+        for i in range(2):
+            for k in range(1, ctx):
+                peer = (c + k) % ctx
+                src, dst = wide_copy(i, peer)
+                remote(src, dst, qo_send.at[i, k], qo_recv.at[i], peer, t).wait_send()
+
+    @pl.when(origin)
+    def dense_sent():
+        def one(n, none):
+            for i in range(2):
+                await_bytes(dense_outs[i], d_send.at[i])
+            return none
+
+        lax.fori_loop(1, ctx * tp, one, 0)
+
+    def settle(step, none):
+        for sub in range(SUB):
+            for way in range(2):
+                hop(way, step, sub).wait_send()
+        return none
+
+    lax.fori_loop(0, tp - 1, settle, 0)
+
+
+def exchange(q, o, k, v, ctx, tp):
+    tokens = q.shape[0]
+    width = q.shape[1] // ctx
+    thin = k.shape[1] // ctx
+    rows = GROUP_SIZE * T // tp
+    anywhere = pl.BlockSpec(memory_space=pl.ANY)
+    dma = pltpu.SemaphoreType.DMA
+    shape = lambda *dims: jax.ShapeDtypeStruct(dims, BF16)
+    return pl.pallas_call(
+        functools.partial(exchange_kernel, ctx, tp),
+        in_specs=[anywhere] * 4,
+        out_specs=[anywhere] * 6,
+        out_shape=[
+            shape(ctx * tokens, width), shape(ctx * tokens, width),
+            shape(tp * ctx * tokens, thin), shape(tp * ctx * tokens, thin),
+            shape(rows, thin), shape(rows, thin),
+        ],
+        scratch_shapes=[
+            dma((2, ctx)), dma((2,)),
+            dma((2, tp - 1, SUB)), dma((2, tp - 1, SUB)),
+            dma((2, ctx)), dma((2,)), dma((2,)), dma((2,)),
+        ],
+        compiler_params=pltpu.CompilerParams(
+            collective_id=2, has_side_effects=True, vmem_limit_bytes=48 * 1024 * 1024
+        ),
+    )(q, o, k, v)
+
+
 def per_device(queries, key_tensor, value_tensor, output_gradient, key_blocks, slot_valid):
     ctx = lax.axis_size("ctx")
     tp = lax.axis_size("tp")
-    tokens = queries.shape[0]
-    pieces = tokens // T
-    heads = KEY_HEADS // ctx
-    rows = GROUP_SIZE * T // tp
-    swap = functools.partial(lax.all_to_all, axis_name="ctx", tiled=True)
-    kv = jnp.concatenate(
-        [key_tensor.reshape(tokens, ctx, heads * D), value_tensor.reshape(tokens, ctx, heads * D)], axis=2
-    ).reshape(tokens, ctx * 2 * heads * D)
-    kv = swap(kv, split_axis=1, concat_axis=0)
-    kv = lax.all_gather(kv, "tp", axis=0, tiled=True)
-    q = swap(queries, split_axis=1, concat_axis=0)
-    o = swap(output_gradient, split_axis=1, concat_axis=0)
-
-    def spread(a):
-        a = a[:T].reshape(T, heads, GROUP_SIZE, D).transpose(2, 0, 1, 3).reshape(GROUP_SIZE * T, heads * D)
-        return lax.all_to_all(a, "tp", split_axis=0, concat_axis=0, tiled=True)[:rows]
-
+    pieces = queries.shape[0] // T
     table, live, keep = tables(key_blocks, slot_valid, ctx, tp, pieces)
-    dq, dk, dv, dqd = gradients(table, live, keep, q, o, kv, spread(q), spread(o))
+    q, o, k, v, qd, od = exchange(queries, output_gradient, key_tensor, value_tensor, ctx, tp)
+    dq, dk, dv, dqd = gradients(table, live, keep, q, o, k, v, qd, od)
     return tuple(send_back(dq, dqd, dk, dv, ctx, tp))
 
 

time: 251 us -> 221 us (0.88)
  Pallas kernels: 115 us -> 205 us
  waiting for transfers between devices: 61.9 us -> 0 us
  starting transfers between devices: 19.5 us -> 0 us
  local copies, waits for them, and re-layouts: 27 us -> 13.5 us
  between operations: 14.1 us -> 0.67 us
  blocking collectives: 12 us -> 0 us
    all_to_all x4 -> x0, waiting for transfers between devices: 61.9 us -> none  [the longest x1 23.3 us: per_device(): o = swap(output_gradient, split_axis=1, concat_axis=0)]
    pallas_call x0 -> x1, Pallas kernels: none -> 55.7 us  [exchange(): pl.pallas_call(functools.partial(exchange_kernel, ctx, tp), in_specs=[any...]
    pallas_call x1, Pallas kernels: 71 us -> 105 us  [send_back(): pl.pallas_call(functools.partial(return_kernel, ctx, tp), in_specs=[anywh...]
    all_to_all x4 -> x0, starting transfers between devices: 19.5 us -> none  [the longest x2 9.51 us: spread(): lax.all_to_all(a, 'tp', split_axis=0, concat_axis=0, tiled=True)[:rows]]
    all_to_all x1 -> x0, blocking collectives: 12 us -> none  [per_device(): kv = swap(kv, split_axis=1, concat_axis=0)]
    all_to_all x4 -> x0, local copies, waits for them, and re-layouts: 8.83 us -> none  [the longest x1 3.98 us: per_device(): o = swap(output_gradient, split_axis=1, concat_axis=0)]
    slice x4 -> x0, local copies, waits for them, and re-layouts: 3.23 us -> none  [the longest x2 2.11 us: spread(): lax.all_to_all(a, 'tp', split_axis=0, concat_axis=0, tiled=True)[:rows]]
    unnamed x17 -> x21, local copies, waits for them, and re-layouts: 11.9 us -> 11.2 us
  transfers between devices with their start and end apart: 5 -> 0, of which waited for: 4 -> 0; matrix products, arithmetic and copies ran while one was open for 8% -> 0% of each run, Pallas kernels for 0% -> 0%
where the time goes in v3:
time: 221 us; the launch traced here: 220 us
  Pallas kernels  205 us (93%)
  local copies, waits for them, and re-layouts  13.5 us (6%)
    pallas_call x1, Pallas kernels, send_back(): pl.pallas_call(functools.partial(return_kernel, ctx, tp), in_specs=[anywh...  105 us
    pallas_call x1, Pallas kernels, exchange(): pl.pallas_call(functools.partial(exchange_kernel, ctx, tp), in_specs=[any...  55.7 us
    pallas_call x1, Pallas kernels, gradients(): pl.pallas_call(grad_kernel, grid_spec=pltpu.PrefetchScalarGridSpec(num_sc...  43.9 us
    unnamed x21, local copies, waits for them, and re-layouts  11.2 us

profile of v3, /device:TPU:1, one launch (start us, length us, event | category | flops | bytes accessed | tf_op | source)
XLA Modules:
  0.0 220.2 jit_solution(14755216490064122786)
XLA Ops:
  0.6 0.6 compare_convert_fusion.keep
  1.2 0.8 reshape.17
  2.0 0.8 reshape.19
  2.8 0.1 constant_dynamic-slice_fusion
  2.8 0.1 copy.12
  2.9 0.7 reshape_reshape.3.live
  3.6 0.1 copy.11
  3.7 0.1 reshape.18
  3.8 0.6 fusion.1.table
  4.4 0.0 copy-start.1
  4.4 0.9 copy-done.1
  5.4 0.0 copy-start.2
  5.4 0.9 copy-done.2
  6.3 55.7 %shard_map.85 = (bf16[512,2048]{1,0:T(8,128)(2,1)S(1)}, bf16[512,2048]{1,0:T(8,128)(2,1)S(1)}, bf16[4096,256]{1,0:T(8,128)(2,1)}, bf16[4096,256]{1,0:T(8,128)(2,...) custom-call(bf16[128,8192]{1,0:T(8,128)(2,1)} %q_ref.1, bf16[128,8192]{1,0:T(8,128)(2,1)} %o_ref.1, ...), custom_call_target="tpu_custom_call" | custom-call | tf_op jit(solution)/shard_map/pallas_call | solution.py:588
  62.0 0.0 copy-start.4
  62.0 1.3 copy-done.4
  63.3 0.0 copy-start.5
  63.3 1.3 copy-done.5
  64.6 0.0 copy-start.6
  64.6 0.6 copy-done.6
  65.3 0.0 copy-start.7
  65.3 0.6 copy-done.7
  65.9 43.9 %shard_map.86 = (bf16[512,2048]{1,0:T(8,128)(2,1)}, bf16[4096,256]{1,0:T(8,128)(2,1)}, bf16[4096,256]{1,0:T(8,128)(2,1)}, bf16[128,256]{1,0:T(8,128)(2,1)}) custom-call(s32[32]{0:T(128)} %fusion.1.table, s32[32]{0:T(128)} %reshape_reshape.3.live, s32[4]{0:T(128)} %compare_convert_fusion.keep, bf16[512,2048]{1,0:T(8,128)(2,1)} %copy-done.4, ...), custom_call_target="tpu_custom_call" | custom-call | flops 13421772800 | bytes 14680064 | tf_op jit(solution)/shard_map/pallas_call | solution.py:154
  109.8 0.0 copy-start
  109.8 1.6 copy-done
  111.3 0.0 copy-start.3
  111.3 0.8 copy-done.3
  112.2 105.3 %shard_map.87 = (bf16[128,8192]{1,0:T(8,128)(2,1)S(1)}, bf16[128,1024]{1,0:T(8,128)(2,1)S(1)}, bf16[128,1024]{1,0:T(8,128)(2,1)S(1)}) custom-call(bf16[512,2048]{1,0:T(8,128)(2,1)S(1)} %copy-done, bf16[128,256]{1,0:T(8,128)(2,1)S(1)} %copy-done.3, bf16[4096,256]{1,0:T(8,128)(2,1)} %get-tuple-element.21.dk_ref, bf16[4096,256]{1,0:T(8,128)(2,1)} %get-tuple-element.22.dv_ref), custom_call_target="tpu_custom_call" | custom-call | tf_op jit(solution)/shard_map/pallas_call | solution.py:409
  217.5 1.3 copy.16
  218.8 0.7 copy.17
  219.5 0.7 copy.18
Async XLA Ops:
  4.4 0.9 copy-start.1
  5.4 0.9 copy-start.2
  62.0 1.3 copy-start.4
  63.3 1.3 copy-start.5
  64.6 0.6 copy-start.6
  65.3 0.6 copy-start.7
  109.8 1.6 copy-start
  111.3 0.8 copy-start.3

commit v4 on v3

--- a/solution.py
+++ b/solution.py
@@ -229,29 +229,31 @@
     pl.semaphore_signal(sem, inc=1, device_id=(c, t), device_id_type=pl.DeviceIdType.MESH)
 
 
-def meet(c, t, ctx, tp, before, after):
+def meet(c, t, ctx, tp, before, after, spread):
     barrier = pltpu.get_barrier_semaphore()
     for k in range(1, ctx):
         signal(barrier, (c + k) % ctx, t)
     signal(barrier, c, before)
     signal(barrier, c, after)
-    origin = c * tp + t == 0
-
-    @pl.when(origin)
+    hub_c = 0 if spread else c
+    hub = (c * tp + t == 0) if spread else (t == 0)
+    count = ctx * tp if spread else tp
+
+    @pl.when(hub)
     def greet():
         def one(i, none):
-            signal(barrier, i // tp, i % tp)
+            signal(barrier, i // tp if spread else c, i % tp)
             return none
 
-        lax.fori_loop(1, ctx * tp, one, 0)
-        pl.semaphore_wait(barrier, ctx + 1 + ctx * tp - 1)
-
-    @pl.when(jnp.logical_not(origin))
+        lax.fori_loop(1, count, one, 0)
+        pl.semaphore_wait(barrier, ctx + 1 + count - 1)
+
+    @pl.when(jnp.logical_not(hub))
     def answer():
-        signal(barrier, 0, 0)
+        signal(barrier, hub_c, 0)
         pl.semaphore_wait(barrier, ctx + 2)
 
-    return origin
+    return hub
 
 
 def remote(src, dst, send, recv, c, t):
@@ -282,7 +284,7 @@
     p = ring_place(t, tp)
     after = ring_owner(p + 1, tp)
     before = ring_owner(p - 1, tp)
-    origin = meet(c, t, ctx, tp, before, after)
+    origin = meet(c, t, ctx, tp, before, after, True)
     ways = ((dk_ref, 1, after), (dv_ref, -1, before))
 
     def own(way, place, sub):
@@ -444,7 +446,7 @@
     p = ring_place(t, tp)
     after = ring_owner(p + 1, tp)
     before = ring_owner(p - 1, tp)
-    origin = meet(c, t, ctx, tp, before, after)
+    hub = meet(c, t, ctx, tp, before, after, False)
     thins = ((k_ref, k_out), (v_ref, v_out))
     wides = ((q_ref, q_out), (o_ref, o_out))
     mine = pl.multiple_of(t * chunk + c * tokens, tokens)
@@ -469,43 +471,26 @@
             dst.at[pl.ds(pl.multiple_of(c * tokens, tokens), tokens), :],
         )
 
-    @pl.when(jnp.logical_not(origin))
-    def wide_start():
-        for i in range(2):
-            for k in range(1, ctx):
-                peer = (c + k) % ctx
-                src, dst = wide_copy(i, peer)
-                remote(src, dst, qo_send.at[i, k], qo_recv.at[i], peer, t).start()
-            src, dst = wide_copy(i, c)
-            pltpu.make_async_copy(src, dst, qo_recv.at[i]).start()
+    for i in range(2):
+        for k in range(1, ctx):
+            peer = (c + k) % ctx
+            src, dst = wide_copy(i, peer)
+            remote(src, dst, qo_send.at[i, k], qo_recv.at[i, c], peer, t).start()
+        src, dst = wide_copy(i, c)
+        pltpu.make_async_copy(src, dst, qo_recv.at[i, c]).start()
 
     rows = qd_out.shape[0]
     dense_outs = (qd_out, od_out)
 
-    def dense(i, h, c_to, t_to):
+    def dense(i, h, t_to):
         first = t_to * rows
-        column = c_to * width + h * (GROUP_SIZE * D) + (first // T) * D
+        column = h * (GROUP_SIZE * D) + (first // T) * D
         return (
-            wides[i][0].at[
+            wides[i][1].at[
                 pl.ds(pl.multiple_of(first % T, rows), rows), pl.ds(pl.multiple_of(column, D), D)
             ],
             dense_outs[i].at[:, h * D:(h + 1) * D],
         )
-
-    @pl.when(origin)
-    def dense_start():
-        def one(n, none):
-            for i in range(2):
-                for h in range(heads):
-                    src, dst = dense(i, h, n // tp, n % tp)
-                    remote(src, dst, d_send.at[i], d_recv.at[i], n // tp, n % tp).start()
-            return none
-
-        lax.fori_loop(1, ctx * tp, one, 0)
-        for i in range(2):
-            for h in range(heads):
-                src, dst = dense(i, h, 0, 0)
-                pltpu.make_async_copy(src, dst, d_recv.at[i]).start()
 
     def hop(way, step, sub):
         place = p - step if way == 0 else p + step
@@ -535,15 +520,28 @@
             hop(way, tp - 2, sub).wait_recv()
 
     for i in range(2):
+        await_bytes(wides[i][1].at[:tokens, :], qo_recv.at[i, 0])
+
+    @pl.when(hub)
+    def dense_start():
+        def one(n, none):
+            for i in range(2):
+                for h in range(heads):
+                    src, dst = dense(i, h, n)
+                    remote(src, dst, d_send.at[i], d_recv.at[i], c, n).start()
+            return none
+
+        lax.fori_loop(1, tp, one, 0)
+        for i in range(2):
+            for h in range(heads):
+                src, dst = dense(i, h, 0)
+                pltpu.make_async_copy(src, dst, d_recv.at[i]).start()
+
+    for i in range(2):
+        for k in range(1, ctx):
+            await_bytes(wides[i][1].at[k * tokens:(k + 1) * tokens, :], qo_recv.at[i, k])
+    for i in range(2):
         await_bytes(dense_outs[i], d_recv.at[i])
-
-        @pl.when(t == 0)
-        def part_rows():
-            await_bytes(wides[i][1].at[tokens:, :], qo_recv.at[i])
-
-        @pl.when(t != 0)
-        def all_rows():
-            await_bytes(wides[i][1], qo_recv.at[i])
 
     for way in range(2):
         for k in range(1, ctx):
@@ -551,22 +549,20 @@
             src, dst = thin_copy(way, peer)
             remote(src, dst, kv_send.at[way, k], kv_recv.at[way], peer, t).wait_send()
 
-    @pl.when(jnp.logical_not(origin))
-    def wide_sent():
-        for i in range(2):
-            for k in range(1, ctx):
-                peer = (c + k) % ctx
-                src, dst = wide_copy(i, peer)
-                remote(src, dst, qo_send.at[i, k], qo_recv.at[i], peer, t).wait_send()
-
-    @pl.when(origin)
+    for i in range(2):
+        for k in range(1, ctx):
+            peer = (c + k) % ctx
+            src, dst = wide_copy(i, peer)
+            remote(src, dst, qo_send.at[i, k], qo_recv.at[i, c], peer, t).wait_send()
+
+    @pl.when(hub)
     def dense_sent():
         def one(n, none):
             for i in range(2):
                 await_bytes(dense_outs[i], d_send.at[i])
             return none
 
-        lax.fori_loop(1, ctx * tp, one, 0)
+        lax.fori_loop(1, tp, one, 0)
 
     def settle(step, none):
         for sub in range(SUB):
@@ -597,7 +593,7 @@
         scratch_shapes=[
             dma((2, ctx)), dma((2,)),
             dma((2, tp - 1, SUB)), dma((2, tp - 1, SUB)),
-            dma((2, ctx)), dma((2,)), dma((2,)), dma((2,)),
+            dma((2, ctx)), dma((2, ctx)), dma((2,)), dma((2,)),
         ],
         compiler_params=pltpu.CompilerParams(
             collective_id=2, has_side_effects=True, vmem_limit_bytes=48 * 1024 * 1024

time: 221 us -> 191 us (0.86)
  Pallas kernels: 205 us -> 174 us
    pallas_call x1, Pallas kernels: 105 us -> 61.8 us  [send_back(): pl.pallas_call(functools.partial(return_kernel, ctx, tp), in_specs=[anywh...]
    pallas_call x1, Pallas kernels: 55.7 us -> 68.7 us  [exchange(): pl.pallas_call(functools.partial(exchange_kernel, ctx, tp), in_specs=[any...]
where the time goes in v4:
time: 191 us; the launch traced here: 190 us
  Pallas kernels  174 us (91%)
  local copies, waits for them, and re-layouts  13.5 us (7%)
    pallas_call x1, Pallas kernels, exchange(): pl.pallas_call(functools.partial(exchange_kernel, ctx, tp), in_specs=[any...  68.7 us
    pallas_call x1, Pallas kernels, send_back(): pl.pallas_call(functools.partial(return_kernel, ctx, tp), in_specs=[anywh...  61.8 us
    pallas_call x1, Pallas kernels, gradients(): pl.pallas_call(grad_kernel, grid_spec=pltpu.PrefetchScalarGridSpec(num_sc...  43.8 us
    unnamed x21, local copies, waits for them, and re-layouts  11.2 us

profile of v4, /device:TPU:1, one launch (start us, length us, event | category | flops | bytes accessed | tf_op | source)
XLA Modules:
  0.0 189.7 jit_solution(8912737107824032390)
XLA Ops:
  0.6 0.6 compare_convert_fusion.keep
  1.2 0.8 reshape.17
  2.0 0.8 reshape.19
  2.8 0.1 constant_dynamic-slice_fusion
  2.8 0.1 copy.12
  2.9 0.7 reshape_reshape.3.live
  3.6 0.1 copy.11
  3.7 0.1 reshape.18
  3.8 0.6 fusion.1.table
  4.4 0.0 copy-start.1
  4.4 0.9 copy-done.1
  5.4 0.0 copy-start.2
  5.4 0.9 copy-done.2
  6.3 68.7 %shard_map.85 = (bf16[512,2048]{1,0:T(8,128)(2,1)S(1)}, bf16[512,2048]{1,0:T(8,128)(2,1)S(1)}, bf16[4096,256]{1,0:T(8,128)(2,1)}, bf16[4096,256]{1,0:T(8,128)(2,...) custom-call(bf16[128,8192]{1,0:T(8,128)(2,1)} %q_ref.1, bf16[128,8192]{1,0:T(8,128)(2,1)} %o_ref.1, ...), custom_call_target="tpu_custom_call" | custom-call | tf_op jit(solution)/shard_map/pallas_call | solution.py:584
  75.0 0.0 copy-start.4
  75.0 1.3 copy-done.4
  76.3 0.0 copy-start.5
  76.3 1.3 copy-done.5
  77.6 0.0 copy-start.6
  77.6 0.6 copy-done.6
  78.3 0.0 copy-start.7
  78.3 0.6 copy-done.7
  78.9 43.8 %shard_map.86 = (bf16[512,2048]{1,0:T(8,128)(2,1)}, bf16[4096,256]{1,0:T(8,128)(2,1)}, bf16[4096,256]{1,0:T(8,128)(2,1)}, bf16[128,256]{1,0:T(8,128)(2,1)}) custom-call(s32[32]{0:T(128)} %fusion.1.table, s32[32]{0:T(128)} %reshape_reshape.3.live, s32[4]{0:T(128)} %compare_convert_fusion.keep, bf16[512,2048]{1,0:T(8,128)(2,1)} %copy-done.4, ...), custom_call_target="tpu_custom_call" | custom-call | flops 13421772800 | bytes 14680064 | tf_op jit(solution)/shard_map/pallas_call | solution.py:154
  122.8 0.0 copy-start
  122.8 1.6 copy-done
  124.3 0.0 copy-start.3
  124.3 0.8 copy-done.3
  125.2 61.8 %shard_map.87 = (bf16[128,8192]{1,0:T(8,128)(2,1)S(1)}, bf16[128,1024]{1,0:T(8,128)(2,1)S(1)}, bf16[128,1024]{1,0:T(8,128)(2,1)S(1)}) custom-call(bf16[512,2048]{1,0:T(8,128)(2,1)S(1)} %copy-done, bf16[128,256]{1,0:T(8,128)(2,1)S(1)} %copy-done.3, bf16[4096,256]{1,0:T(8,128)(2,1)} %get-tuple-element.21.dk_ref, bf16[4096,256]{1,0:T(8,128)(2,1)} %get-tuple-element.22.dv_ref), custom_call_target="tpu_custom_call" | custom-call | tf_op jit(solution)/shard_map/pallas_call | solution.py:411
  187.0 1.3 copy.16
  188.3 0.7 copy.17
  189.0 0.7 copy.18
Async XLA Ops:
  4.4 0.9 copy-start.1
  5.4 0.9 copy-start.2
  75.0 1.3 copy-start.4
  76.3 1.3 copy-start.5
  77.6 0.6 copy-start.6
  78.3 0.6 copy-start.7
  122.8 1.6 copy-start
  124.3 0.8 copy-start.3
